TPU v7x, 32 devices: a whole 2x2x4 slice. The times are simulated.
32 devices in a mesh: groups: 2 (over y), lon: 4 (over z), lat: 2 (over x), cl: 2 (over core).
Axes of the slice: x: 2, y: 2, z: 4, core: 2. Of those that a mesh axis runs over, the one named last changes fastest.
Arguments:
- ocean_state: float32 [8, 32, 8, 1024], P('groups', None, 'lat', ('lon', 'cl')), parts along dimension 0, may hold values from -6 to 6
- cotangent: float32 [8, 32, 8, 1024], P('groups', None, 'lat', ('lon', 'cl')), parts along dimension 0, may hold values from -6 to 6
- diffusivity: float32 [32, 8, 1024], P(None, 'lat', ('lon', 'cl')), may hold values from 0.02 to 0.24
- east_peclet: float32 [32, 8, 1024], P(None, 'lat', ('lon', 'cl')), may hold values from -0.9 to 0.9
- north_peclet: float32 [32, 8, 1024], P(None, 'lat', ('lon', 'cl')), may hold values from -0.9 to 0.9
- sea_mask: int32 [8, 1024], P('lat', ('lon', 'cl')), may hold values 0 or 1
- depth_levels: int32 [8, 1024], P('lat', ('lon', 'cl')), may hold values from 1 to 32
- owner_table: int32 [2, 8, 512, 1], P('lat', ('lon', 'cl')), may hold values from 0 to 7; in each aligned block of 512 rows (0 to 511, 512 to 1023, ..., all dimensions but the last counted through in order) at most 128 rows name the same one
- w_in: bfloat16 [8, 128, 256], P(('lon', 'lat')), may hold values from -0.5 to 0.5
- w_mid: bfloat16 [8, 1, 256, 256], P(('lon', 'lat')), may hold values from -0.375 to 0.375
- w_out: bfloat16 [8, 256, 128], P(('lon', 'lat')), may hold values from -0.375 to 0.375
Outputs:
- advected: float32 [8, 32, 8, 1024], P('groups', None, 'lat', ('lon', 'cl')), parts along dimension 0
- tendency: bfloat16 [8, 32, 8, 1024], P('groups', None, 'lat', ('lon', 'cl')), parts along dimension 0
- state_grad: float32 [8, 32, 8, 1024], P('groups', None, 'lat', ('lon', 'cl')), parts along dimension 0
- grad_w_in: float32 [16, 128, 256], P(('groups', 'lon', 'lat')), parts along dimension 0
- grad_w_mid: float32 [16, 1, 256, 256], P(('groups', 'lon', 'lat')), parts along dimension 0
- grad_w_out: float32 [16, 256, 128], P(('groups', 'lon', 'lat')), parts along dimension 0
There are 2 independent parts, one for each index of `groups`. A program takes and returns all parts, laid end to end along the dimension named above; an argument that names none is the same for every part. Nothing has to cross between parts.
Inputs may be any that keep to these rules, and one draw needn't show every extreme that they name: `owner_table`: in each device's block of 512 columns of the table, no region is named more than 128 times.
All inputs are finite; a program needn't handle non-finite values. No bound on the sum of `sea_mask` on one device may be relied on, other than what follows from the above.
Results may differ from a plain program's by a relative error of at most 0.0068.
Values may be sent and summed in bfloat16 or wider, within the bound.
A program may use at most 64 MiB of HBM per device.

v0:
```python
import jax
import jax.numpy as jnp
from jax import lax
from jax.sharding import PartitionSpec as P

STEPS = 2


def padded_2(value, sides, width, wrap):
    for axis, dim in sides:
        size, length = (lax.axis_size(axis), value.shape[dim])
        up = [(i, (i + 1) % size) for i in range(size if wrap else size - 1)]
        down = [(j, i) for i, j in up]
        last = lax.slice_in_dim(value, length - width, length, axis=dim)
        leading = lax.slice_in_dim(value, 0, width, axis=dim)
        before = lax.ppermute(last, axis, up)
        after = lax.ppermute(leading, axis, down)
        value = jnp.concatenate([before, value, after], axis=dim)
    return value


def build_table(diffusivity, east_peclet, north_peclet, sea_mask, depth_levels):
    levels = lax.broadcasted_iota(jnp.int32, diffusivity.shape, 0)
    active = (levels < depth_levels[None]).astype(jnp.float32) * sea_mask[None].astype(jnp.float32)
    return jnp.stack(
        [
            diffusivity * (1.0 - east_peclet),
            diffusivity * (1.0 + east_peclet),
            diffusivity * (1.0 - north_peclet),
            diffusivity * (1.0 + north_peclet),
            4.0 * diffusivity,
            active,
        ]
    )


def with_rims(grid_values, width):
    padded = padded_2(grid_values, (("lat", 2),), width, False)
    return padded_2(padded, ((("lon", "cl"), 3),), width, True)


def advance(padded, coefficients):
    inner_coef = coefficients[:, :, 1:-1, 1:-1]
    interior = padded[:, :, 1:-1, 1:-1]
    change = inner_coef[0] * padded[:, :, 1:-1, 2:] + inner_coef[1] * padded[:, :, 1:-1, :-2]
    change = (
        change + inner_coef[2] * padded[:, :, 2:, 1:-1] + inner_coef[3] * padded[:, :, :-2, 1:-1]
    )
    return interior + inner_coef[5] * (change - inner_coef[4] * interior)


def retreat(padded, coefficients):
    pushed = coefficients[5] * padded
    summed = padded[:, :, 1:-1, 1:-1] - (coefficients[4] * pushed)[:, :, 1:-1, 1:-1]
    summed = (
        summed
        + (coefficients[0] * pushed)[:, :, 1:-1, :-2]
        + (coefficients[1] * pushed)[:, :, 1:-1, 2:]
    )
    summed = (
        summed
        + (coefficients[2] * pushed)[:, :, :-2, 1:-1]
        + (coefficients[3] * pushed)[:, :, 2:, 1:-1]
    )
    return summed


def sweep_steps(grid_values, coefficients, update):
    for number in range(STEPS):
        grid_values = update(with_rims(grid_values, 1), coefficients)
    return grid_values


def project(left, right):
    return jnp.dot(left, right, preferred_element_type=jnp.float32)


def project_back(left, right):
    return lax.dot_general(
        left, right, (((1,), (1,)), ((), ())), preferred_element_type=jnp.float32
    )


def contract_rows(left, right):
    return lax.dot_general(
        left, right, (((0,), (0,)), ((), ())), preferred_element_type=jnp.float32
    )


def closure_pass(inputs, pushed, w_in, w_mid, w_out):
    slopes = []
    layers = [inputs]
    shaped = jnp.tanh(project(inputs, w_in))
    slopes.append(1.0 - shaped * shaped)
    acting = shaped.astype(jnp.bfloat16)
    layers.append(acting)
    layer_index = 0
    shaped = jnp.tanh(project(acting, w_mid[layer_index]))
    slopes.append(1.0 - shaped * shaped)
    acting = shaped.astype(jnp.bfloat16)
    layers.append(acting)
    raw_tend = project(acting, w_out).astype(jnp.bfloat16)
    grad_out = contract_rows(acting, pushed)
    backward = project_back(pushed, w_out)
    mid_grads = []
    for layer_index in reversed(range(w_mid.shape[0])):
        deltas = (backward * slopes[layer_index + 1]).astype(jnp.bfloat16)
        mid_grads.append(contract_rows(layers[layer_index + 1], deltas))
        backward = project_back(deltas, w_mid[layer_index])
    deltas = (backward * slopes[0]).astype(jnp.bfloat16)
    grad_in = contract_rows(inputs, deltas)
    back_in = project_back(deltas, w_in).astype(jnp.bfloat16)
    return (raw_tend, back_in, grad_in, jnp.stack(mid_grads[::-1]), grad_out)


def on_device(
    ocean_state,
    cotangent,
    diffusivity,
    east_peclet,
    north_peclet,
    sea_mask,
    depth_levels,
    owner_table,
    w_in,
    w_mid,
    w_out,
):
    coefficients = build_table(diffusivity, east_peclet, north_peclet, sea_mask, depth_levels)
    active = coefficients[5]
    rim_width = 1
    coef_rims = with_rims(coefficients, rim_width)
    advected = sweep_steps(ocean_state, coef_rims, advance)
    features = ocean_state.shape[0] * ocean_state.shape[1]
    columns = ocean_state.shape[2] * ocean_state.shape[3]
    experts = lax.axis_size(("lon", "lat"))
    capacity = 2 * columns // experts
    owners = owner_table.reshape(columns)
    one_hot = (owners[:, None] == lax.broadcasted_iota(jnp.int32, (columns, experts), 1)).astype(
        jnp.int32
    )
    rank_in = jnp.sum(jnp.cumsum(one_hot, axis=0) * one_hot, axis=1) - 1
    slot_index = owners * capacity + rank_in
    col_inputs = advected.reshape(features, columns).T.astype(jnp.bfloat16)
    col_pushed = (active[None] * cotangent).reshape(features, columns).T.astype(jnp.bfloat16)
    empty = jnp.zeros((experts * capacity, features), jnp.bfloat16)
    send_inputs = empty.at[slot_index].set(col_inputs)
    send_pushed = empty.at[slot_index].set(col_pushed)
    got_inputs, got_pushed = (
        lax.all_to_all(send_inputs, ("lon", "lat"), split_axis=0, concat_axis=0, tiled=True),
        lax.all_to_all(send_pushed, ("lon", "lat"), split_axis=0, concat_axis=0, tiled=True),
    )
    raw_tend, back_in, grad_in, grad_mid, grad_out = closure_pass(
        got_inputs, got_pushed, w_in[0], w_mid[0], w_out[0]
    )
    grad_in, grad_mid, grad_out = lax.psum((grad_in, grad_mid, grad_out), "cl")
    ret_tend, ret_back = (
        lax.all_to_all(raw_tend, ("lon", "lat"), split_axis=0, concat_axis=0, tiled=True),
        lax.all_to_all(back_in, ("lon", "lat"), split_axis=0, concat_axis=0, tiled=True),
    )
    tend_grid = ret_tend[slot_index].T.reshape(ocean_state.shape)
    back_grid = ret_back[slot_index].T.reshape(ocean_state.shape)
    tendency = (active[None] * tend_grid.astype(jnp.float32)).astype(jnp.bfloat16)
    adjoint_start = cotangent + back_grid.astype(jnp.float32)
    state_grad = sweep_steps(adjoint_start, coef_rims, retreat)
    return (advected, tendency, state_grad, grad_in[None], grad_mid[None], grad_out[None])


def solution(mesh):
    return jax.shard_map(
        on_device,
        mesh=mesh,
        in_specs=(
            P("groups", None, "lat", ("lon", "cl")),
            P("groups", None, "lat", ("lon", "cl")),
            P(None, "lat", ("lon", "cl")),
            P(None, "lat", ("lon", "cl")),
            P(None, "lat", ("lon", "cl")),
            P("lat", ("lon", "cl")),
            P("lat", ("lon", "cl")),
            P("lat", ("lon", "cl"), None, None),
            P(("lon", "lat"), None, None),
            P(("lon", "lat"), None, None, None),
            P(("lon", "lat"), None, None),
        ),
        out_specs=(
            P("groups", None, "lat", ("lon", "cl")),
            P("groups", None, "lat", ("lon", "cl")),
            P("groups", None, "lat", ("lon", "cl")),
            P(("groups", "lon", "lat"), None, None),
            P(("groups", "lon", "lat"), None, None, None),
            P(("groups", "lon", "lat"), None, None),
        ),
        check_vma=False,
    )
```

profile of v0, /device:TPU:1, one launch (start us, length us, event | category | flops | bytes accessed | tf_op | source)
XLA Modules:
  0.0 205.3 jit_solution(14176597876775129136)
XLA Ops:
  9.7 4.0 %collective-permute-start = (f32[4,32,1,128]{3,2,1,0:T(1,128)S(1)}, f32[4,32,1,128]{3,2,1,0:T(1,128)S(1)}, u32[]{:S(2)}, u32[]{:S(2)}) collective-permute-start(f32[4,32,1,128]{3,2,1,0:T(1,128)S(1)} %get-tuple-element.44), channel_id=1, source_target_pairs={{0,2},{1,3},{4,6},{5,7},{8,10},{9,11},{12,14},{13,15},{16,18},{17,... | collective-permute-start | bytes 196616 | tf_op jit(solution)/shard_map/ppermute | solution.py:16
  21.5 2.4 %collective-permute-start.3 = (f32[4,32,6,1]{3,2,1,0:T(8,128)S(1)}, f32[4,32,6,1]{3,2,1,0:T(8,128)S(1)}, u32[]{:S(2)}, u32[]{:S(2)}) collective-permute-start(f32[4,32,6,1]{3,2,1,0:T(8,128)S(1)} %get-tuple-element.34), channel_id=1, source_target_pairs={{0,1},{1,4},{4,5},{5,8},{8,9},{9,12},{12,13},{13,0},{2,3},{3,6},{6... | collective-permute-start | bytes 9224 | tf_op jit(solution)/shard_map/ppermute | solution.py:16
  24.2 8.1 %collective-permute-done.2 = f32[4,32,6,1]{3,2,1,0:T(8,128)S(1)} collective-permute-done((f32[4,32,6,1]{3,2,1,0:T(8,128)S(1)}, f32[4,32,6,1]{3,2,1,0:T(8,128)S(1)}, u32[]{:S(2)}, u32[]{:S(2)}) %collective-permute-start.2) | collective-permute-done | bytes 3104 | tf_op jit(solution)/shard_map/ppermute | solution.py:17
  32.3 1.8 collective-permute-done.3
  36.6 4.0 %collective-permute-start.4 = (f32[4,32,1,128]{3,2,1,0:T(1,128)S(1)}, f32[4,32,1,128]{3,2,1,0:T(1,128)S(1)}, u32[]{:S(2)}, u32[]{:S(2)}) collective-permute-start(f32[4,32,1,128]{3,2,1,0:T(1,128)S(1)} %get-tuple-element.42), channel_id=1, source_target_pairs={{0,2},{1,3},{4,6},{5,7},{8,10},{9,11},{12,14},{13,15},{16,18},{17,... | collective-permute-start | bytes 196616 | tf_op jit(solution)/shard_map/ppermute | solution.py:16
  42.3 6.0 %collective-permute-start.6 = (f32[4,32,6,1]{3,2,1,0:T(8,128)S(1)}, f32[4,32,6,1]{3,2,1,0:T(8,128)S(1)}, u32[]{:S(2)}, u32[]{:S(2)}) collective-permute-start(f32[4,32,6,1]{3,2,1,0:T(8,128)S(1)} %get-tuple-element.31), channel_id=1, source_target_pairs={{1,0},{4,1},{5,4},{8,5},{9,8},{12,9},{13,12},{0,13},{3,2},{6,3},{7... | collective-permute-start | bytes 9224 | tf_op jit(solution)/shard_map/ppermute | solution.py:17
  48.3 5.0 %collective-permute-done.6 = f32[4,32,6,1]{3,2,1,0:T(8,128)S(1)} collective-permute-done((f32[4,32,6,1]{3,2,1,0:T(8,128)S(1)}, f32[4,32,6,1]{3,2,1,0:T(8,128)S(1)}, u32[]{:S(2)}, u32[]{:S(2)}) %collective-permute-start.6) | collective-permute-done | bytes 3104 | tf_op jit(solution)/shard_map/ppermute | solution.py:17
  53.3 6.5 %collective-permute-done.7 = f32[4,32,6,1]{3,2,1,0:T(8,128)S(1)} collective-permute-done((f32[4,32,6,1]{3,2,1,0:T(8,128)S(1)}, f32[4,32,6,1]{3,2,1,0:T(8,128)S(1)}, u32[]{:S(2)}, u32[]{:S(2)}) %collective-permute-start.7) | collective-permute-done | bytes 3104 | tf_op jit(solution)/shard_map/ppermute | solution.py:16
  59.9 1.7 fusion.51
  61.7 1.8 scatter_custom_fusion
  63.6 16.2 %all_to_all.48 = bf16[8,128,128]{2,1,0:T(8,128)(2,1)S(1)} all-to-all(bf16[8,128,128]{2,1,0:T(8,128)(2,1)S(1)} %bitcast.102), channel_id=1, replica_groups=mesh['groups'=2,'lon'=4,'lat'=2,'cl'=2] {'lon','lat'}, dimensions={0} | all-to-all | bytes 524288 | tf_op jit(solution)/shard_map/all_to_all | solution.py:150
  81.9 3.4 %all-to-all-start.1 = ((bf16[8,128,128]{2,1,0:T(8,128)(2,1)}), bf16[8,128,128]{2,1,0:T(8,128)(2,1)S(1)}, u32[]{:S(2)}, u32[]{:S(2)}) async-start(bf16[8,128,128]{2,1,0:T(8,128)(2,1)} %bitcast.13), calls=%async_computation.1 | async-start | bytes 524288 | tf_op jit(solution)/shard_map/all_to_all | solution.py:158
  85.3 7.6 %all-to-all-done.1 = bf16[8,128,128]{2,1,0:T(8,128)(2,1)S(1)} async-done(((bf16[8,128,128]{2,1,0:T(8,128)(2,1)}), bf16[8,128,128]{2,1,0:T(8,128)(2,1)S(1)}, u32[]{:S(2)}, u32[]{:S(2)}) %all-to-all-start.1) | async-done | bytes 262176 | tf_op jit(solution)/shard_map/all_to_all | solution.py:158
  95.5 2.4 %scatter_custom_fusion.1 = bf16[1024,128]{1,0:T(8,128)(2,1)} fusion(s32[512]{0:T(512)S(1)} %bitcast.111, bf16[128,512]{0,1:T(8,128)(2,1)S(1)} %copy.65, bf16[]{:T(256)} %constant.6.clone.1), kind=kCustom, calls=%fused_computation.95 | custom fusion | bytes 393218 | tf_op jit(solution)/shard_map/scatter | solution.py:148
  97.9 4.6 %all-to-all-start.2 = ((bf16[8,128,128]{2,1,0:T(8,128)(2,1)}), bf16[8,128,128]{2,1,0:T(8,128)(2,1)S(1)}, u32[]{:S(2)}, u32[]{:S(2)}) async-start(bf16[8,128,128]{2,1,0:T(8,128)(2,1)} %bitcast.17), calls=%async_computation.2 | async-start | bytes 524288 | tf_op jit(solution)/shard_map/all_to_all | solution.py:151
  102.6 3.4 %collective-permute-start.8 = (f32[6,32,1,128]{3,1,2,0:T(8,128)S(1)}, f32[6,32,1,128]{3,1,2,0:T(8,128)S(1)}, u32[]{:S(2)}, u32[]{:S(2)}) collective-permute-start(f32[6,32,1,128]{3,1,2,0:T(8,128)S(1)} %get-tuple-element.35), channel_id=1, source_target_pairs={{0,2},{1,3},{4,6},{5,7},{8,10},{9,11},{12,14},{13,15},{16,18},{17,... | collective-permute-start | bytes 294920 | tf_op jit(solution)/shard_map/ppermute | solution.py:16
  108.2 3.6 %collective-permute-done.9 = f32[6,32,1,128]{3,1,2,0:T(8,128)S(1)} collective-permute-done((f32[6,32,1,128]{3,1,2,0:T(8,128)S(1)}, f32[6,32,1,128]{3,1,2,0:T(8,128)S(1)}, u32[]{:S(2)}, u32[]{:S(2)}) %collective-permute-start.9) | collective-permute-done | bytes 98336 | tf_op jit(solution)/shard_map/ppermute | solution.py:17
  115.0 3.8 %all-to-all-start.3 = ((bf16[8,128,128]{2,1,0:T(8,128)(2,1)}), bf16[8,128,128]{2,1,0:T(8,128)(2,1)S(1)}, u32[]{:S(2)}, u32[]{:S(2)}) async-start(bf16[8,128,128]{2,1,0:T(8,128)(2,1)} %bitcast.101), calls=%async_computation.3 | async-start | bytes 524288 | tf_op jit(solution)/shard_map/all_to_all | solution.py:159
  121.4 4.9 %collective-permute-start.10 = (f32[6,32,6,1]{1,3,2,0:T(1,128)S(1)}, f32[6,32,6,1]{1,3,2,0:T(1,128)S(1)}, u32[]{:S(2)}, u32[]{:S(2)}) collective-permute-start(f32[6,32,6,1]{1,3,2,0:T(1,128)S(1)} %copy.77), channel_id=1, source_target_pairs={{0,1},{1,4},{4,5},{5,8},{8,9},{9,12},{12,13},{13,0},{2,3},{3,6},{6... | collective-permute-start | bytes 13832 | tf_op jit(solution)/shard_map/ppermute | solution.py:16
  128.2 2.9 %collective-permute-done.11 = f32[6,32,6,1]{1,3,2,0:T(1,128)S(1)} collective-permute-done((f32[6,32,6,1]{1,3,2,0:T(1,128)S(1)}, f32[6,32,6,1]{1,3,2,0:T(1,128)S(1)}, u32[]{:S(2)}, u32[]{:S(2)}) %collective-permute-start.11) | collective-permute-done | bytes 4640 | tf_op jit(solution)/shard_map/ppermute | solution.py:17
  138.6 1.8 copy.66
  140.4 1.7 reshape.101
  143.3 3.1 %collective-permute-start.12 = (f32[4,32,1,128]{3,2,1,0:T(1,128)S(1)}, f32[4,32,1,128]{3,2,1,0:T(1,128)S(1)}, u32[]{:S(2)}, u32[]{:S(2)}) collective-permute-start(f32[4,32,1,128]{3,2,1,0:T(1,128)S(1)} %get-tuple-element.39), channel_id=1, source_target_pairs={{0,2},{1,3},{4,6},{5,7},{8,10},{9,11},{12,14},{13,15},{16,18},{17,... | collective-permute-start | bytes 196616 | tf_op jit(solution)/shard_map/ppermute | solution.py:16
  148.7 2.7 %collective-permute-done.13 = f32[4,32,1,128]{3,2,1,0:T(1,128)S(1)} collective-permute-done((f32[4,32,1,128]{3,2,1,0:T(1,128)S(1)}, f32[4,32,1,128]{3,2,1,0:T(1,128)S(1)}, u32[]{:S(2)}, u32[]{:S(2)}) %collective-permute-start.13) | collective-permute-done | bytes 65568 | tf_op jit(solution)/shard_map/ppermute | solution.py:17
  151.8 1.9 collective-permute-start.14
  155.1 6.2 %collective-permute-done.14 = f32[4,32,6,1]{3,2,1,0:T(8,128)S(1)} collective-permute-done((f32[4,32,6,1]{3,2,1,0:T(8,128)S(1)}, f32[4,32,6,1]{3,2,1,0:T(8,128)S(1)}, u32[]{:S(2)}, u32[]{:S(2)}) %collective-permute-start.14) | collective-permute-done | bytes 3104 | tf_op jit(solution)/shard_map/ppermute | solution.py:16
  161.3 5.4 %collective-permute-done.15 = f32[4,32,6,1]{3,2,1,0:T(8,128)S(1)} collective-permute-done((f32[4,32,6,1]{3,2,1,0:T(8,128)S(1)}, f32[4,32,6,1]{3,2,1,0:T(8,128)S(1)}, u32[]{:S(2)}, u32[]{:S(2)}) %collective-permute-start.15) | collective-permute-done | bytes 3104 | tf_op jit(solution)/shard_map/ppermute | solution.py:17
  172.1 2.7 %collective-permute-done.17 = f32[4,32,1,128]{3,2,1,0:T(1,128)S(1)} collective-permute-done((f32[4,32,1,128]{3,2,1,0:T(1,128)S(1)}, f32[4,32,1,128]{3,2,1,0:T(1,128)S(1)}, u32[]{:S(2)}, u32[]{:S(2)}) %collective-permute-start.17) | collective-permute-done | bytes 65568 | tf_op jit(solution)/shard_map/ppermute | solution.py:17
  175.8 4.2 %collective-permute-start.19 = (f32[4,32,6,1]{3,2,1,0:T(8,128)S(1)}, f32[4,32,6,1]{3,2,1,0:T(8,128)S(1)}, u32[]{:S(2)}, u32[]{:S(2)}) collective-permute-start(f32[4,32,6,1]{3,2,1,0:T(8,128)S(1)} %get-tuple-element.28), channel_id=1, source_target_pairs={{1,0},{4,1},{5,4},{8,5},{9,8},{12,9},{13,12},{0,13},{3,2},{6,3},{7... | collective-permute-start | bytes 9224 | tf_op jit(solution)/shard_map/ppermute | solution.py:17
  180.0 2.0 collective-permute-done.18
  182.0 3.1 %collective-permute-done.19 = f32[4,32,6,1]{3,2,1,0:T(8,128)S(1)} collective-permute-done((f32[4,32,6,1]{3,2,1,0:T(8,128)S(1)}, f32[4,32,6,1]{3,2,1,0:T(8,128)S(1)}, u32[]{:S(2)}, u32[]{:S(2)}) %collective-permute-start.19) | collective-permute-done | bytes 3104 | tf_op jit(solution)/shard_map/ppermute | solution.py:17
  187.4 6.2 %all-reduce.3.cloned.1.call-done = (f32[1,128,256]{2,1,0:T(8,128)}, f32[1,1,256,256]{3,2,1,0:T(8,128)}, f32[1,256,128]{2,1,0:T(8,128)}) async-done(((f32[1,128,256]{2,1,0:T(8,128)}, f32[1,1,256,256]{3,2,1,0:T(8,128)}, f32[1,256,128]{2,1,0:T(8,128)}), (f32[1,128,256]{2,1,0:T(8,128)}, f32[1,1,256,256]{3,2,1,0:T(8,128)}, f32[1,256,128]{2,1,0:T(8,128)})) %all-reduce.3.cloned.1.call-update) | async-done | bytes 524304 | tf_op jit(solution)/shard_map/psum | solution.py:156
  (157 shorter events, 55.3 us)
Async XLA Ops:
  7.2 72.9 %copy-start = (bf16[1,1,256,256]{3,2,1,0:T(8,128)(2,1)S(1)}, bf16[1,1,256,256]{3,2,1,0:T(8,128)(2,1)}, u32[]{:S(2)}) copy-start(bf16[1,1,256,256]{3,2,1,0:T(8,128)(2,1)} %param.20) | copy-start | bytes 393220
  7.2 12.9 %copy-start.10 = (f32[4,32,4,128]{3,2,1,0:T(4,128)S(1)}, f32[4,32,4,128]{3,2,1,0:T(4,128)}, u32[]{:S(2)}) copy-start(f32[4,32,4,128]{3,2,1,0:T(4,128)} %param.11) | copy-start | bytes 786436
  7.2 12.6 %copy-start.24 = (s32[4,128]{1,0:T(4,128)S(1)}, s32[4,128]{1,0:T(4,128)}, u32[]{:S(2)}) copy-start(s32[4,128]{1,0:T(4,128)} %param.17) | copy-start | bytes 6148
  8.4 11.7 %collective-permute-start.1 = (f32[4,32,1,128]{3,2,1,0:T(1,128)S(1)}, f32[4,32,1,128]{3,2,1,0:T(1,128)S(1)}, u32[]{:S(2)}, u32[]{:S(2)}) collective-permute-start(f32[4,32,1,128]{3,2,1,0:T(1,128)S(1)} %get-tuple-element.43), channel_id=1, source_target_pairs={{2,0},{3,1},{6,4},{7,5},{10,8},{11,9},{14,12},{15,13},{18,16},{19,... | collective-permute-start | bytes 196616 | tf_op jit(solution)/shard_map/ppermute | solution.py:17
  9.7 10.4 %collective-permute-start = (f32[4,32,1,128]{3,2,1,0:T(1,128)S(1)}, f32[4,32,1,128]{3,2,1,0:T(1,128)S(1)}, u32[]{:S(2)}, u32[]{:S(2)}) collective-permute-start(f32[4,32,1,128]{3,2,1,0:T(1,128)S(1)} %get-tuple-element.44), channel_id=1, source_target_pairs={{0,2},{1,3},{4,6},{5,7},{8,10},{9,11},{12,14},{13,15},{16,18},{17,... | collective-permute-start | bytes 196616 | tf_op jit(solution)/shard_map/ppermute | solution.py:16
  20.5 11.9 %collective-permute-start.2 = (f32[4,32,6,1]{3,2,1,0:T(8,128)S(1)}, f32[4,32,6,1]{3,2,1,0:T(8,128)S(1)}, u32[]{:S(2)}, u32[]{:S(2)}) collective-permute-start(f32[4,32,6,1]{3,2,1,0:T(8,128)S(1)} %get-tuple-element.33), channel_id=1, source_target_pairs={{1,0},{4,1},{5,4},{8,5},{9,8},{12,9},{13,12},{0,13},{3,2},{6,3},{7... | collective-permute-start | bytes 9224 | tf_op jit(solution)/shard_map/ppermute | solution.py:17
  21.5 12.7 %collective-permute-start.3 = (f32[4,32,6,1]{3,2,1,0:T(8,128)S(1)}, f32[4,32,6,1]{3,2,1,0:T(8,128)S(1)}, u32[]{:S(2)}, u32[]{:S(2)}) collective-permute-start(f32[4,32,6,1]{3,2,1,0:T(8,128)S(1)} %get-tuple-element.34), channel_id=1, source_target_pairs={{0,1},{1,4},{4,5},{5,8},{8,9},{9,12},{12,13},{13,0},{2,3},{3,6},{6... | collective-permute-start | bytes 9224 | tf_op jit(solution)/shard_map/ppermute | solution.py:16
  35.3 5.3 %collective-permute-start.5 = (f32[4,32,1,128]{3,2,1,0:T(1,128)S(1)}, f32[4,32,1,128]{3,2,1,0:T(1,128)S(1)}, u32[]{:S(2)}, u32[]{:S(2)}) collective-permute-start(f32[4,32,1,128]{3,2,1,0:T(1,128)S(1)} %get-tuple-element.41), channel_id=1, source_target_pairs={{2,0},{3,1},{6,4},{7,5},{10,8},{11,9},{14,12},{15,13},{18,16},{19,... | collective-permute-start | bytes 196616 | tf_op jit(solution)/shard_map/ppermute | solution.py:17
  36.6 5.3 %collective-permute-start.4 = (f32[4,32,1,128]{3,2,1,0:T(1,128)S(1)}, f32[4,32,1,128]{3,2,1,0:T(1,128)S(1)}, u32[]{:S(2)}, u32[]{:S(2)}) collective-permute-start(f32[4,32,1,128]{3,2,1,0:T(1,128)S(1)} %get-tuple-element.42), channel_id=1, source_target_pairs={{0,2},{1,3},{4,6},{5,7},{8,10},{9,11},{12,14},{13,15},{16,18},{17,... | collective-permute-start | bytes 196616 | tf_op jit(solution)/shard_map/ppermute | solution.py:16
  42.3 11.1 %collective-permute-start.6 = (f32[4,32,6,1]{3,2,1,0:T(8,128)S(1)}, f32[4,32,6,1]{3,2,1,0:T(8,128)S(1)}, u32[]{:S(2)}, u32[]{:S(2)}) collective-permute-start(f32[4,32,6,1]{3,2,1,0:T(8,128)S(1)} %get-tuple-element.31), channel_id=1, source_target_pairs={{1,0},{4,1},{5,4},{8,5},{9,8},{12,9},{13,12},{0,13},{3,2},{6,3},{7... | collective-permute-start | bytes 9224 | tf_op jit(solution)/shard_map/ppermute | solution.py:17
  48.3 11.6 %collective-permute-start.7 = (f32[4,32,6,1]{3,2,1,0:T(8,128)S(1)}, f32[4,32,6,1]{3,2,1,0:T(8,128)S(1)}, u32[]{:S(2)}, u32[]{:S(2)}) collective-permute-start(f32[4,32,6,1]{3,2,1,0:T(8,128)S(1)} %get-tuple-element.32), channel_id=1, source_target_pairs={{0,1},{1,4},{4,5},{5,8},{8,9},{9,12},{12,13},{13,0},{2,3},{3,6},{6... | collective-permute-start | bytes 9224 | tf_op jit(solution)/shard_map/ppermute | solution.py:16
  61.6 18.2 %copy-start.19 = (bf16[1,128,256]{2,1,0:T(8,128)(2,1)S(1)}, bf16[1,128,256]{2,1,0:T(8,128)(2,1)}, u32[]{:S(2)}) copy-start(bf16[1,128,256]{2,1,0:T(8,128)(2,1)} %param.19) | copy-start | bytes 196612
  81.9 11.1 %all-to-all-start.1 = ((bf16[8,128,128]{2,1,0:T(8,128)(2,1)}), bf16[8,128,128]{2,1,0:T(8,128)(2,1)S(1)}, u32[]{:S(2)}, u32[]{:S(2)}) async-start(bf16[8,128,128]{2,1,0:T(8,128)(2,1)} %bitcast.13), calls=%async_computation.1 | async-start | bytes 524288 | tf_op jit(solution)/shard_map/all_to_all | solution.py:158
  97.9 14.6 %copy-start.22 = (bf16[1,256,128]{2,1,0:T(8,128)(2,1)S(1)}, bf16[1,256,128]{2,1,0:T(8,128)(2,1)}, u32[]{:S(2)}) copy-start(bf16[1,256,128]{2,1,0:T(8,128)(2,1)} %param.21) | copy-start | bytes 196612
  97.9 14.5 %all-to-all-start.2 = ((bf16[8,128,128]{2,1,0:T(8,128)(2,1)}), bf16[8,128,128]{2,1,0:T(8,128)(2,1)S(1)}, u32[]{:S(2)}, u32[]{:S(2)}) async-start(bf16[8,128,128]{2,1,0:T(8,128)(2,1)} %bitcast.17), calls=%async_computation.2 | async-start | bytes 524288 | tf_op jit(solution)/shard_map/all_to_all | solution.py:151
  102.6 5.6 %collective-permute-start.8 = (f32[6,32,1,128]{3,1,2,0:T(8,128)S(1)}, f32[6,32,1,128]{3,1,2,0:T(8,128)S(1)}, u32[]{:S(2)}, u32[]{:S(2)}) collective-permute-start(f32[6,32,1,128]{3,1,2,0:T(8,128)S(1)} %get-tuple-element.35), channel_id=1, source_target_pairs={{0,2},{1,3},{4,6},{5,7},{8,10},{9,11},{12,14},{13,15},{16,18},{17,... | collective-permute-start | bytes 294920 | tf_op jit(solution)/shard_map/ppermute | solution.py:16
  106.0 5.8 %collective-permute-start.9 = (f32[6,32,1,128]{3,1,2,0:T(8,128)S(1)}, f32[6,32,1,128]{3,1,2,0:T(8,128)S(1)}, u32[]{:S(2)}, u32[]{:S(2)}) collective-permute-start(f32[6,32,1,128]{3,1,2,0:T(8,128)S(1)} %get-tuple-element.36), channel_id=1, source_target_pairs={{2,0},{3,1},{6,4},{7,5},{10,8},{11,9},{14,12},{15,13},{18,16},{19,... | collective-permute-start | bytes 294920 | tf_op jit(solution)/shard_map/ppermute | solution.py:17
  115.0 21.5 %all-to-all-start.3 = ((bf16[8,128,128]{2,1,0:T(8,128)(2,1)}), bf16[8,128,128]{2,1,0:T(8,128)(2,1)S(1)}, u32[]{:S(2)}, u32[]{:S(2)}) async-start(bf16[8,128,128]{2,1,0:T(8,128)(2,1)} %bitcast.101), calls=%async_computation.3 | async-start | bytes 524288 | tf_op jit(solution)/shard_map/all_to_all | solution.py:159
  118.8 74.9 %all-reduce.3.cloned.1.call-start = ((), (), s32[]{:S(2)}) async-start(), calls=%async_computation.4 | async-start | bytes 1048576 | tf_op jit(solution)/shard_map/psum | solution.py:156
  121.4 6.5 %collective-permute-start.10 = (f32[6,32,6,1]{1,3,2,0:T(1,128)S(1)}, f32[6,32,6,1]{1,3,2,0:T(1,128)S(1)}, u32[]{:S(2)}, u32[]{:S(2)}) collective-permute-start(f32[6,32,6,1]{1,3,2,0:T(1,128)S(1)} %copy.77), channel_id=1, source_target_pairs={{0,1},{1,4},{4,5},{5,8},{8,9},{9,12},{12,13},{13,0},{2,3},{3,6},{6... | collective-permute-start | bytes 13832 | tf_op jit(solution)/shard_map/ppermute | solution.py:16
  127.6 3.4 %collective-permute-start.11 = (f32[6,32,6,1]{1,3,2,0:T(1,128)S(1)}, f32[6,32,6,1]{1,3,2,0:T(1,128)S(1)}, u32[]{:S(2)}, u32[]{:S(2)}) collective-permute-start(f32[6,32,6,1]{1,3,2,0:T(1,128)S(1)} %copy.78), channel_id=1, source_target_pairs={{1,0},{4,1},{5,4},{8,5},{9,8},{12,9},{13,12},{0,13},{3,2},{6,3},{7... | collective-permute-start | bytes 13832 | tf_op jit(solution)/shard_map/ppermute | solution.py:17
  143.3 5.5 %collective-permute-start.12 = (f32[4,32,1,128]{3,2,1,0:T(1,128)S(1)}, f32[4,32,1,128]{3,2,1,0:T(1,128)S(1)}, u32[]{:S(2)}, u32[]{:S(2)}) collective-permute-start(f32[4,32,1,128]{3,2,1,0:T(1,128)S(1)} %get-tuple-element.39), channel_id=1, source_target_pairs={{0,2},{1,3},{4,6},{5,7},{8,10},{9,11},{12,14},{13,15},{16,18},{17,... | collective-permute-start | bytes 196616 | tf_op jit(solution)/shard_map/ppermute | solution.py:16
  146.4 5.0 %collective-permute-start.13 = (f32[4,32,1,128]{3,2,1,0:T(1,128)S(1)}, f32[4,32,1,128]{3,2,1,0:T(1,128)S(1)}, u32[]{:S(2)}, u32[]{:S(2)}) collective-permute-start(f32[4,32,1,128]{3,2,1,0:T(1,128)S(1)} %get-tuple-element.40), channel_id=1, source_target_pairs={{2,0},{3,1},{6,4},{7,5},{10,8},{11,9},{14,12},{15,13},{18,16},{19,... | collective-permute-start | bytes 196616 | tf_op jit(solution)/shard_map/ppermute | solution.py:17
  151.8 9.5 %collective-permute-start.14 = (f32[4,32,6,1]{3,2,1,0:T(8,128)S(1)}, f32[4,32,6,1]{3,2,1,0:T(8,128)S(1)}, u32[]{:S(2)}, u32[]{:S(2)}) collective-permute-start(f32[4,32,6,1]{3,2,1,0:T(8,128)S(1)} %get-tuple-element.29), channel_id=1, source_target_pairs={{0,1},{1,4},{4,5},{5,8},{8,9},{9,12},{12,13},{13,0},{2,3},{3,6},{6... | collective-permute-start | bytes 9224 | tf_op jit(solution)/shard_map/ppermute | solution.py:16
  153.7 13.1 %collective-permute-start.15 = (f32[4,32,6,1]{3,2,1,0:T(8,128)S(1)}, f32[4,32,6,1]{3,2,1,0:T(8,128)S(1)}, u32[]{:S(2)}, u32[]{:S(2)}) collective-permute-start(f32[4,32,6,1]{3,2,1,0:T(8,128)S(1)} %get-tuple-element.30), channel_id=1, source_target_pairs={{1,0},{4,1},{5,4},{8,5},{9,8},{12,9},{13,12},{0,13},{3,2},{6,3},{7... | collective-permute-start | bytes 9224 | tf_op jit(solution)/shard_map/ppermute | solution.py:17
  155.1 12.7 %copy-start.13 = (f32[32,4,128]{2,1,0:T(4,128)S(1)}, f32[32,4,128]{2,1,0:T(4,128)}, u32[]{:S(2)}) copy-start(f32[32,4,128]{2,1,0:T(4,128)} %copy.95) | copy-start | bytes 196612
  155.1 12.7 %copy-start.14 = (f32[32,4,128]{2,1,0:T(4,128)S(1)}, f32[32,4,128]{2,1,0:T(4,128)}, u32[]{:S(2)}) copy-start(f32[32,4,128]{2,1,0:T(4,128)} %copy.96) | copy-start | bytes 196612
  155.1 12.7 %copy-start.15 = (f32[32,4,128]{2,1,0:T(4,128)S(1)}, f32[32,4,128]{2,1,0:T(4,128)}, u32[]{:S(2)}) copy-start(f32[32,4,128]{2,1,0:T(4,128)} %copy.97) | copy-start | bytes 196612
  168.5 3.6 %collective-permute-start.16 = (f32[4,32,1,128]{3,2,1,0:T(1,128)S(1)}, f32[4,32,1,128]{3,2,1,0:T(1,128)S(1)}, u32[]{:S(2)}, u32[]{:S(2)}) collective-permute-start(f32[4,32,1,128]{3,2,1,0:T(1,128)S(1)} %get-tuple-element.37), channel_id=1, source_target_pairs={{0,2},{1,3},{4,6},{5,7},{8,10},{9,11},{12,14},{13,15},{16,18},{17,... | collective-permute-start | bytes 196616 | tf_op jit(solution)/shard_map/ppermute | solution.py:16
  169.8 5.0 %collective-permute-start.17 = (f32[4,32,1,128]{3,2,1,0:T(1,128)S(1)}, f32[4,32,1,128]{3,2,1,0:T(1,128)S(1)}, u32[]{:S(2)}, u32[]{:S(2)}) collective-permute-start(f32[4,32,1,128]{3,2,1,0:T(1,128)S(1)} %get-tuple-element.38), channel_id=1, source_target_pairs={{2,0},{3,1},{6,4},{7,5},{10,8},{11,9},{14,12},{15,13},{18,16},{19,... | collective-permute-start | bytes 196616 | tf_op jit(solution)/shard_map/ppermute | solution.py:17
  175.2 6.8 %collective-permute-start.18 = (f32[4,32,6,1]{3,2,1,0:T(8,128)S(1)}, f32[4,32,6,1]{3,2,1,0:T(8,128)S(1)}, u32[]{:S(2)}, u32[]{:S(2)}) collective-permute-start(f32[4,32,6,1]{3,2,1,0:T(8,128)S(1)} %get-tuple-element.27), channel_id=1, source_target_pairs={{0,1},{1,4},{4,5},{5,8},{8,9},{9,12},{12,13},{13,0},{2,3},{3,6},{6... | collective-permute-start | bytes 9224 | tf_op jit(solution)/shard_map/ppermute | solution.py:16
  175.8 9.2 %collective-permute-start.19 = (f32[4,32,6,1]{3,2,1,0:T(8,128)S(1)}, f32[4,32,6,1]{3,2,1,0:T(8,128)S(1)}, u32[]{:S(2)}, u32[]{:S(2)}) collective-permute-start(f32[4,32,6,1]{3,2,1,0:T(8,128)S(1)} %get-tuple-element.28), channel_id=1, source_target_pairs={{1,0},{4,1},{5,4},{8,5},{9,8},{12,9},{13,12},{0,13},{3,2},{6,3},{7... | collective-permute-start | bytes 9224 | tf_op jit(solution)/shard_map/ppermute | solution.py:17
  (17 other events, 63.3 us)
Sparse Core Ops, SparseCore 0:
  172.2 21.3 all-reduce.2
where the time goes:
time: 209 us; the launch traced here: 205 us
  waiting for transfers between devices  66.1 us (32%)
  starting transfers between devices  55.7 us (27%)
  local copies, waits for them, and re-layouts  28.6 us (14%)
  other arithmetic  17.8 us (9%)
  blocking collectives  16.2 us (8%)
  between operations  14.7 us (7%)
  matrix products  6.18 us (3%)
    ppermute x10, waiting for transfers between devices, padded_2(): after = lax.ppermute(leading, axis, down)  33.5 us
    ppermute x10, starting transfers between devices, padded_2(): before = lax.ppermute(last, axis, up)  25.6 us
    ppermute x10, waiting for transfers between devices, padded_2(): before = lax.ppermute(last, axis, up)  18.7 us
    ppermute x10, starting transfers between devices, padded_2(): after = lax.ppermute(leading, axis, down)  18.3 us
    all_to_all x1, blocking collectives, on_device(): lax.all_to_all(send_inputs, ('lon', 'lat'), split_axis=0, concat_axis=0,...  16.2 us
    unnamed x62, local copies, waits for them, and re-layouts  11.7 us
    all_to_all x1, waiting for transfers between devices, on_device(): lax.all_to_all(raw_tend, ('lon', 'lat'), split_axis=0, concat_axis=0, til...  7.63 us
    psum x1, waiting for transfers between devices, on_device(): grad_in, grad_mid, grad_out = lax.psum((grad_in, grad_mid, grad_out), 'cl')  6.25 us
  transfers between devices with their start and end apart: 24, of which 16 were waited for; matrix products, arithmetic and copies ran while one was open for 11% of the time, Pallas kernels for 0%

commit v1 on v0

--- a/solution.py
+++ b/solution.py
@@ -1,6 +1,10 @@
+import functools
+
 import jax
 import jax.numpy as jnp
 from jax import lax
+from jax.experimental import pallas as pl
+from jax.experimental.pallas import tpu as pltpu
 from jax.sharding import PartitionSpec as P
 
 STEPS = 2
@@ -166,9 +170,296 @@
     return (advected, tendency, state_grad, grad_in[None], grad_mid[None], grad_out[None])
 
 
+MESH = pl.DeviceIdType.MESH
+VMEM_BYTES = 48 * 1024 * 1024
+
+
+def matmul(left, right, contract):
+    return lax.dot_general(
+        left, right, (((contract[0],), (contract[1],)), ((), ())),
+        preferred_element_type=jnp.float32,
+    )
+
+
+def tile_kernel(
+    n_lon, n_lat, n_cl, cap,
+    x_ref, cot_ref, diff_ref, ep_ref, np_ref, sea_ref, dep_ref, own_ref, wi_ref, wm_ref, wo_ref,
+    adv_ref, tend_ref, sg_ref, gi_ref, gm_ref, go_ref,
+    d8, tmp, hal, lat_s, lat_r, lon_s, lon_r, pt, snd, rcv, gis, gms, gos, gir, gmr, gor,
+    lat_ss, lat_rs, lon_ss, lon_rs, a2a_ss, a2a_rs, g_ss, g_rs,
+):
+    experts = n_lon * n_lat
+    lon, lat, cl = lax.axis_index("lon"), lax.axis_index("lat"), lax.axis_index("cl")
+    ring = n_lon * n_cl
+    place = lon * n_cl + cl
+    east, west = (place + 1) % ring, (place + ring - 1) % ring
+    east_id = {"lon": east // n_cl, "cl": east % n_cl}
+    west_id = {"lon": west // n_cl, "cl": west % n_cl}
+    lat_id = {"lat": 1 - lat}
+    cl_id = {"cl": 1 - cl}
+    me = lon * n_lat + lat
+    partners = [(me + d) % experts for d in range(experts)]
+    partner_ids = [{"lon": p // n_lat, "lat": p % n_lat} for p in partners]
+
+    barrier = pltpu.get_barrier_semaphore()
+    for other in partner_ids[1:] + [east_id, west_id]:
+        pl.semaphore_signal(barrier, inc=1, device_id=other, device_id_type=MESH)
+
+    rows, wide = x_ref.shape
+    tiles = rows // 8
+    fields = rows // diff_ref.shape[0]
+    feats = rows // 4
+    cube = (tiles, 8, wide)
+    four = (fields, tiles // fields, 8, wide)
+    lane = lax.broadcasted_iota(jnp.int32, cube, 2)
+    tile = lax.broadcasted_iota(jnp.int32, cube, 0)
+    row = lax.broadcasted_iota(jnp.int32, cube, 1) % 4
+    on_tile = lane == tile
+    south = jnp.full(cube, lat, jnp.int32) == 0
+
+    d8[0, 0:4], d8[0, 4:8] = sea_ref[...], sea_ref[...]
+    d8[1, 0:4], d8[1, 4:8] = dep_ref[...], dep_ref[...]
+    flat = (tiles // fields, 8, wide)
+    level = 2 * lax.broadcasted_iota(jnp.int32, flat, 0) + (
+        lax.broadcasted_iota(jnp.int32, flat, 1) // 4
+    )
+    diff = diff_ref[...].reshape(flat)
+    ep, np_ = ep_ref[...].reshape(flat), np_ref[...].reshape(flat)
+    active = (level < d8[1][None]).astype(jnp.float32) * d8[0][None].astype(jnp.float32)
+    c_e, c_w = (diff * (1.0 - ep))[None], (diff * (1.0 + ep))[None]
+    c_n, c_s = (diff * (1.0 - np_))[None], (diff * (1.0 + np_))[None]
+    c_0, act = (4.0 * diff)[None], active[None]
+
+    def pack(value, side):
+        return jnp.sum(jnp.where(on_tile, value[:, :, side : side + 1], 0.0), axis=0)
+
+    def unpack(packed):
+        return jnp.sum(jnp.where(on_tile, packed[None], 0.0), axis=2, keepdims=True)
+
+    def send_edges(number, to_e, to_w, to_n, to_s):
+        tmp[...] = jnp.where(south, to_n, to_s).reshape(rows, wide)
+        pick = jnp.full((feats, wide), lat, jnp.int32) == 0
+        lat_s[number] = jnp.where(
+            pick, tmp[pl.ds(3, feats, stride=4), :], tmp[pl.ds(0, feats, stride=4), :]
+        )
+        lon_s[number, 0] = pack(to_e, wide - 1)
+        lon_s[number, 1] = pack(to_w, 0)
+        copies = [
+            pltpu.make_async_remote_copy(
+                lat_s.at[number], lat_r.at[number], lat_ss.at[number], lat_rs.at[number],
+                device_id=lat_id, device_id_type=MESH,
+            ),
+            pltpu.make_async_remote_copy(
+                lon_s.at[number, 0], lon_r.at[number, 0],
+                lon_ss.at[number, 0], lon_rs.at[number, 0],
+                device_id=east_id, device_id_type=MESH,
+            ),
+            pltpu.make_async_remote_copy(
+                lon_s.at[number, 1], lon_r.at[number, 1],
+                lon_ss.at[number, 1], lon_rs.at[number, 1],
+                device_id=west_id, device_id_type=MESH,
+            ),
+        ]
+        for copy in copies:
+            copy.start()
+        return copies
+
+    def shifted(number, copies, to_e, to_w, to_n, to_s):
+        for copy in copies:
+            copy.wait()
+        from_w = jnp.where(lane == 0, unpack(lon_r[number, 0]), pltpu.roll(to_e, 1, 2))
+        from_e = jnp.where(
+            lane == wide - 1, unpack(lon_r[number, 1]), pltpu.roll(to_w, wide - 1, 2)
+        )
+        hal[pl.ds(0, feats, stride=4), :] = lat_r[number]
+        hal[pl.ds(3, feats, stride=4), :] = lat_r[number]
+        edge = hal[...].reshape(cube)
+        from_s = jnp.where(row == 0, jnp.where(south, 0.0, edge), pltpu.roll(to_n, 1, 1))
+        from_n = jnp.where(row == 3, jnp.where(south, edge, 0.0), pltpu.roll(to_s, 7, 1))
+        return [v.reshape(four) for v in (from_w, from_e, from_s, from_n)]
+
+    def exchange(kind):
+        copies = []
+        for d in range(1, experts):
+            copies.append(
+                pltpu.make_async_remote_copy(
+                    snd.at[kind, partners[d]], rcv.at[kind, me],
+                    a2a_ss.at[kind, d], a2a_rs.at[kind, d],
+                    device_id=partner_ids[d], device_id_type=MESH,
+                )
+            )
+            copies[-1].start()
+        rcv[kind, me] = snd[kind, me]
+        return copies
+
+    def arrived(kind, copies):
+        for copy in copies:
+            copy.wait()
+        return jnp.concatenate([rcv[kind, e] for e in range(experts)], axis=1)
+
+    def columns_of(ref):
+        return jnp.concatenate(
+            [ref[pl.ds(i, feats, stride=4), :] for i in range(4)], axis=1
+        ).astype(jnp.bfloat16)
+
+    def to_slots(kind, columns):
+        slots = matmul(columns, pt[...], (1, 1)).astype(jnp.bfloat16)
+        for e in range(experts):
+            snd[kind, e] = slots[:, e * cap : (e + 1) * cap]
+
+    def to_grid(slots):
+        columns = matmul(slots, pt[...], (1, 0))
+        for i in range(4):
+            tmp[pl.ds(i, feats, stride=4), :] = columns[:, i * wide : (i + 1) * wide]
+        return tmp[...].reshape(four)
+
+    count = 4 * wide
+    owners = jnp.concatenate([own_ref[i : i + 1, :] for i in range(4)], axis=1)
+    hot = (owners == lax.broadcasted_iota(jnp.int32, (experts, count), 0)).astype(jnp.float32)
+    before = (
+        lax.broadcasted_iota(jnp.int32, (count, count), 0)
+        < lax.broadcasted_iota(jnp.int32, (count, count), 1)
+    ).astype(jnp.float32).astype(jnp.bfloat16)
+    earlier = matmul(hot.astype(jnp.bfloat16), before, (1, 0))
+    rank = jnp.sum(hot * earlier, axis=0, keepdims=True)
+    slot = owners * cap + rank.astype(jnp.int32)
+    pt[...] = (
+        lax.broadcasted_iota(jnp.int32, (experts * cap, count), 0) == slot
+    ).astype(jnp.float32).astype(jnp.bfloat16)
+
+    cot = cot_ref[...].reshape(four)
+    tmp[...] = (act * cot).reshape(rows, wide)
+    to_slots(0, columns_of(tmp))
+
+    pl.semaphore_wait(barrier, experts - 1 + 2)
+
+    state = x_ref[...].reshape(four)
+    sent = []
+    for number in range(STEPS):
+        whole = state.reshape(cube)
+        copies = send_edges(number, whole, whole, whole, whole)
+        if number == 0:
+            sent = exchange(0)
+        from_w, from_e, from_s, from_n = shifted(number, copies, whole, whole, whole, whole)
+        change = c_e * from_e + c_w * from_w + c_n * from_n + c_s * from_s
+        state = state + act * (change - c_0 * state)
+    adv_ref[...] = state.reshape(rows, wide)
+    to_slots(1, columns_of(adv_ref))
+    sent_in = exchange(1)
+    pushed = arrived(0, sent)
+    back_2 = matmul(wo_ref[...], pushed, (1, 0))
+    inputs = arrived(1, sent_in)
+
+    t_0 = jnp.tanh(matmul(wi_ref[...], inputs, (0, 0)))
+    a_0 = t_0.astype(jnp.bfloat16)
+    t_1 = jnp.tanh(matmul(wm_ref[...], a_0, (0, 0)))
+    a_1 = t_1.astype(jnp.bfloat16)
+    delta_1 = (back_2 * (1.0 - t_1 * t_1)).astype(jnp.bfloat16)
+    back_1 = matmul(wm_ref[...], delta_1, (1, 0))
+    delta_0 = (back_1 * (1.0 - t_0 * t_0)).astype(jnp.bfloat16)
+    back_in = matmul(wi_ref[...], delta_0, (1, 0)).astype(jnp.bfloat16)
+    for e in range(experts):
+        snd[2, e] = back_in[:, e * cap : (e + 1) * cap]
+    sent_back = exchange(2)
+    raw = matmul(wo_ref[...], a_1, (0, 0)).astype(jnp.bfloat16)
+    for e in range(experts):
+        snd[3, e] = raw[:, e * cap : (e + 1) * cap]
+    sent_raw = exchange(3)
+    gis[...] = matmul(inputs, delta_0, (1, 1))
+    gms[...] = matmul(a_0, delta_1, (1, 1))
+    gos[...] = matmul(a_1, pushed, (1, 1))
+    sent_grads = []
+    for i, (src, dst) in enumerate(((gis, gir), (gms, gmr), (gos, gor))):
+        sent_grads.append(
+            pltpu.make_async_remote_copy(
+                src, dst, g_ss.at[i], g_rs.at[i], device_id=cl_id, device_id_type=MESH
+            )
+        )
+        sent_grads[-1].start()
+
+    grad = cot + to_grid(arrived(2, sent_back))
+    for number in range(STEPS, 2 * STEPS):
+        held = act * grad
+        parts = [(c * held).reshape(cube) for c in (c_e, c_w, c_n, c_s)]
+        copies = send_edges(number, *parts)
+        base = grad - c_0 * held
+        if number == 2 * STEPS - 1:
+            tend = arrived(3, sent_raw)
+        from_w, from_e, from_s, from_n = shifted(number, copies, *parts)
+        grad = base + from_w + from_e + from_s + from_n
+    sg_ref[...] = grad.reshape(rows, wide)
+    tend_ref[...] = (act * to_grid(tend)).reshape(rows, wide)
+    for copy in sent_grads:
+        copy.wait()
+    gi_ref[...] = gis[...] + gir[...]
+    gm_ref[...] = gms[...] + gmr[...]
+    go_ref[...] = gos[...] + gor[...]
+
+
+def on_device_fused(
+    ocean_state, cotangent, diffusivity, east_peclet, north_peclet, sea_mask, depth_levels,
+    owner_table, w_in, w_mid, w_out,
+):
+    n_lon, n_lat, n_cl = (lax.axis_size(axis) for axis in ("lon", "lat", "cl"))
+    wide = ocean_state.shape[3]
+    rows = ocean_state.size // wide
+    columns = 4 * wide
+    experts = n_lon * n_lat
+    cap = 2 * columns // experts
+    feats, hidden = w_in.shape[1:]
+    f32, bf16 = jnp.float32, jnp.bfloat16
+    vmem = pl.BlockSpec(memory_space=pltpu.VMEM)
+    flat = lambda v: v.reshape(-1, wide)
+    out = pl.pallas_call(
+        functools.partial(tile_kernel, n_lon, n_lat, n_cl, cap),
+        out_shape=[
+            jax.ShapeDtypeStruct((rows, wide), f32),
+            jax.ShapeDtypeStruct((rows, wide), f32),
+            jax.ShapeDtypeStruct((rows, wide), f32),
+            jax.ShapeDtypeStruct((feats, hidden), f32),
+            jax.ShapeDtypeStruct((hidden, hidden), f32),
+            jax.ShapeDtypeStruct((hidden, feats), f32),
+        ],
+        in_specs=[vmem] * 11,
+        out_specs=[vmem] * 6,
+        scratch_shapes=[
+            pltpu.VMEM((2, 8, wide), jnp.int32),
+            pltpu.VMEM((rows, wide), f32),
+            pltpu.VMEM((rows, wide), f32),
+            pltpu.VMEM((2 * STEPS, feats, wide), f32),
+            pltpu.VMEM((2 * STEPS, feats, wide), f32),
+            pltpu.VMEM((2 * STEPS, 2, 8, wide), f32),
+            pltpu.VMEM((2 * STEPS, 2, 8, wide), f32),
+            pltpu.VMEM((experts * cap, columns), bf16),
+            pltpu.VMEM((4, experts, feats, cap), bf16),
+            pltpu.VMEM((4, experts, feats, cap), bf16),
+        ]
+        + [pltpu.VMEM(s, f32) for s in ((feats, hidden), (hidden, hidden), (hidden, feats))] * 2
+        + [pltpu.SemaphoreType.DMA((2 * STEPS,))] * 2
+        + [pltpu.SemaphoreType.DMA((2 * STEPS, 2))] * 2
+        + [pltpu.SemaphoreType.DMA((4, experts))] * 2
+        + [pltpu.SemaphoreType.DMA((3,))] * 2,
+        compiler_params=pltpu.CompilerParams(
+            collective_id=0, has_side_effects=True, vmem_limit_bytes=VMEM_BYTES
+        ),
+    )(
+        flat(ocean_state), flat(cotangent), flat(diffusivity), flat(east_peclet),
+        flat(north_peclet), sea_mask, depth_levels, flat(owner_table), w_in[0], w_mid[0, 0],
+        w_out[0],
+    )
+    advected, tendency, state_grad, grad_in, grad_mid, grad_out = out
+    shape = ocean_state.shape
+    return (
+        advected.reshape(shape), tendency.astype(bf16).reshape(shape), state_grad.reshape(shape),
+        grad_in[None], grad_mid[None, None], grad_out[None],
+    )
+
+
 def solution(mesh):
+    few = mesh.shape["lat"] == 2 and mesh.shape["cl"] == 2 and 2 < mesh.shape["lon"] <= 4
+    plan = on_device_fused if few else on_device
     return jax.shard_map(
-        on_device,
+        plan,
         mesh=mesh,
         in_specs=(
             P("groups", None, "lat", ("lon", "cl")),

time: 209 us -> 54.4 us (0.26); the launches traced: 205 us -> 54 us
  waiting for transfers between devices: 66.1 us -> 0 us
  starting transfers between devices: 55.7 us -> 0 us
  Pallas kernels: 0 us -> 41.5 us
  local copies, waits for them, and re-layouts: 28.6 us -> 11.1 us
  other arithmetic: 17.8 us -> 0.67 us
  blocking collectives: 16.2 us -> 0 us
  between operations: 14.7 us -> 0.68 us
  matrix products: 6.18 us -> 0 us
    ppermute x20 -> x0, waiting for transfers between devices: 52.2 us -> none  [the longest x10 33.5 us: padded_2(): after = lax.ppermute(leading, axis, down)]
    ppermute x20 -> x0, starting transfers between devices: 43.8 us -> none  [the longest x10 25.6 us: padded_2(): before = lax.ppermute(last, axis, up)]
    pallas_call x0 -> x1, Pallas kernels: none -> 41.5 us  [on_device_fused(): pl.pallas_call(functools.partial(tile_kernel, n_lon, n_lat, n_cl, cap), o...]
    all_to_all x1 -> x0, blocking collectives: 16.2 us -> none  [on_device(): lax.all_to_all(send_inputs, ('lon', 'lat'), split_axis=0, concat_axis=0,...]
    all_to_all x3 -> x0, starting transfers between devices: 11.8 us -> none  [the longest x1 4.62 us: on_device(): lax.all_to_all(send_pushed, ('lon', 'lat'), split_axis=0, concat_axis=0,...]
    all_to_all x3 -> x0, waiting for transfers between devices: 7.63 us -> none  [the longest x1 7.63 us: on_device(): lax.all_to_all(raw_tend, ('lon', 'lat'), split_axis=0, concat_axis=0, til...]
    psum x1 -> x0, waiting for transfers between devices: 6.25 us -> none  [on_device(): grad_in, grad_mid, grad_out = lax.psum((grad_in, grad_mid, grad_out), 'cl')]
    dot_general x9 -> x0, matrix products: 6.18 us -> none  [the longest x3 2.97 us: contract_rows(): lax.dot_general(left, right, (((0,), (0,)), ((), ())), preferred_element_...]
  transfers between devices with their start and end apart: 24 -> 0, of which waited for: 16 -> 0; matrix products, arithmetic and copies ran while one was open for 11% -> 0% of each run, Pallas kernels for 0% -> 0%
where the time goes in v1:
time: 54.4 us; the launch traced here: 54 us
  Pallas kernels  41.5 us (76%)
  local copies, waits for them, and re-layouts  11.1 us (20%)
  between operations  0.68 us (1%)
  other arithmetic  0.67 us (1%)
    pallas_call x1, Pallas kernels, on_device_fused(): pl.pallas_call(functools.partial(tile_kernel, n_lon, n_lat, n_cl, cap), o...  41.5 us
    unnamed x27, local copies, waits for them, and re-layouts  11.1 us

profile of v1, /device:TPU:1, one launch (start us, length us, event | category | flops | bytes accessed | tf_op | source)
XLA Modules:
  0.0 54.0 jit_solution(8907903871061936992)
XLA Ops:
  0.6 0.0 copy-start.10
  0.6 0.0 copy-start.9
  0.7 0.0 copy-start.8
  0.7 0.7 %copy-done.10 = s32[1,1,512,1]{2,3,1,0:T(1,128)S(1)} copy-done((s32[1,1,512,1]{2,3,1,0:T(1,128)S(1)}, s32[1,1,512,1]{2,3,1,0:T(1,128)}, u32[]{:S(2)}) %copy-start.10) | copy-done | bytes 2072
  1.3 0.0 copy-done.9
  1.3 0.0 copy-done.8
  1.4 0.0 copy-start
  1.4 0.9 %copy-done = f32[4,32,4,128]{3,2,1,0:T(4,128)S(1)} copy-done((f32[4,32,4,128]{3,2,1,0:T(4,128)S(1)}, f32[4,32,4,128]{3,2,1,0:T(4,128)}, u32[]{:S(2)}) %copy-start) | copy-done | bytes 262168
  2.3 0.0 copy-start.1
  2.3 0.9 %copy-done.1 = f32[4,32,4,128]{3,2,1,0:T(4,128)S(1)} copy-done((f32[4,32,4,128]{3,2,1,0:T(4,128)S(1)}, f32[4,32,4,128]{3,2,1,0:T(4,128)}, u32[]{:S(2)}) %copy-start.1) | copy-done | bytes 262168
  3.3 0.0 copy-start.2
  3.3 0.9 %copy-done.2 = bf16[1,1,256,256]{3,2,1,0:T(8,128)(2,1)S(1)} copy-done((bf16[1,1,256,256]{3,2,1,0:T(8,128)(2,1)S(1)}, bf16[1,1,256,256]{3,2,1,0:T(8,128)(2,1)}, u32[]{:S(2)}) %copy-start.2) | copy-done | bytes 131096
  4.2 0.0 copy-start.3
  4.2 0.8 %copy-done.3 = f32[32,4,128]{2,1,0:T(4,128)S(1)} copy-done((f32[32,4,128]{2,1,0:T(4,128)S(1)}, f32[32,4,128]{2,1,0:T(4,128)}, u32[]{:S(2)}) %copy-start.3) | copy-done | bytes 65560
  5.0 0.0 copy-start.4
  5.0 0.8 %copy-done.4 = f32[32,4,128]{2,1,0:T(4,128)S(1)} copy-done((f32[32,4,128]{2,1,0:T(4,128)S(1)}, f32[32,4,128]{2,1,0:T(4,128)}, u32[]{:S(2)}) %copy-start.4) | copy-done | bytes 65560
  5.8 0.0 copy-start.5
  5.8 0.8 %copy-done.5 = f32[32,4,128]{2,1,0:T(4,128)S(1)} copy-done((f32[32,4,128]{2,1,0:T(4,128)S(1)}, f32[32,4,128]{2,1,0:T(4,128)}, u32[]{:S(2)}) %copy-start.5) | copy-done | bytes 65560
  6.7 0.0 copy-start.6
  6.7 0.8 %copy-done.6 = bf16[1,128,256]{2,1,0:T(8,128)(2,1)S(1)} copy-done((bf16[1,128,256]{2,1,0:T(8,128)(2,1)S(1)}, bf16[1,128,256]{2,1,0:T(8,128)(2,1)}, u32[]{:S(2)}) %copy-start.6) | copy-done | bytes 65560
  7.5 0.0 copy-start.7
  7.5 0.8 %copy-done.7 = bf16[1,256,128]{2,1,0:T(8,128)(2,1)S(1)} copy-done((bf16[1,256,128]{2,1,0:T(8,128)(2,1)S(1)}, bf16[1,256,128]{2,1,0:T(8,128)(2,1)}, u32[]{:S(2)}) %copy-start.7) | copy-done | bytes 65560
  8.4 41.5 %shard_map.154 = (f32[512,128]{1,0:T(8,128)S(1)}, f32[512,128]{1,0:T(8,128)S(1)}, f32[512,128]{1,0:T(8,128)S(1)}, f32[128,256]{1,0:T(8,128)S(1)}, f32[256,256]{1,0:T(8,128)S(1)}, /*index=5*/f32[256,128]{1,0:T(8,128)S(1)}) custom-call(f32[512,128]{1,0:T(8,128)S(1)} %bitcast.18, f32[512,128]{1,0:T(8,128)S(1)} %bitcast.19, f32[128,128]{1,0:T(8,128)S(1)} %bitcast.23, ...), custom_call_target="tpu_custom_call" | custom-call | tf_op jit(solution)/shard_map/pallas_call | solution.py:413
  49.9 0.7 %convert_element_type.3 = bf16[512,128]{1,0:T(8,128)(2,1)} convert(f32[512,128]{1,0:T(8,128)S(1)} %get-tuple-element.13) | non-fusion elementwise | flops 65536 | bytes 393216 | tf_op jit(solution)/shard_map/convert_element_type | solution.py:453
  50.6 0.7 %copy.22 = f32[4,32,4,128]{3,2,1,0:T(4,128)} copy(f32[4,32,4,128]{3,2,1,0:T(4,128)S(1)} %bitcast.17) | data formatting | bytes 524288
  51.3 0.7 %copy.23 = f32[4,32,4,128]{3,2,1,0:T(4,128)} copy(f32[4,32,4,128]{3,2,1,0:T(4,128)S(1)} %bitcast.16) | data formatting | bytes 524288
  52.0 0.7 %copy.24 = f32[1,128,256]{2,1,0:T(8,128)} copy(f32[1,128,256]{2,1,0:T(8,128)S(1)} %bitcast.22) | data formatting | bytes 262144
  52.6 0.7 %copy.25 = f32[1,1,256,256]{3,2,1,0:T(8,128)} copy(f32[1,1,256,256]{3,2,1,0:T(8,128)S(1)} %bitcast.15) | data formatting | bytes 524288
  53.3 0.7 %copy.26 = f32[1,256,128]{2,1,0:T(8,128)} copy(f32[1,256,128]{2,1,0:T(8,128)S(1)} %bitcast.21) | data formatting | bytes 262144
Async XLA Ops:
  0.6 0.7 %copy-start.10 = (s32[1,1,512,1]{2,3,1,0:T(1,128)S(1)}, s32[1,1,512,1]{2,3,1,0:T(1,128)}, u32[]{:S(2)}) copy-start(s32[1,1,512,1]{2,3,1,0:T(1,128)} %param.18) | copy-start | bytes 6148
  0.6 0.7 %copy-start.9 = (s32[4,128]{1,0:T(4,128)S(1)}, s32[4,128]{1,0:T(4,128)}, u32[]{:S(2)}) copy-start(s32[4,128]{1,0:T(4,128)} %dep_ref.1) | copy-start | bytes 6148
  0.7 0.7 %copy-start.8 = (s32[4,128]{1,0:T(4,128)S(1)}, s32[4,128]{1,0:T(4,128)}, u32[]{:S(2)}) copy-start(s32[4,128]{1,0:T(4,128)} %sea_ref.1) | copy-start | bytes 6148
  1.4 0.9 %copy-start = (f32[4,32,4,128]{3,2,1,0:T(4,128)S(1)}, f32[4,32,4,128]{3,2,1,0:T(4,128)}, u32[]{:S(2)}) copy-start(f32[4,32,4,128]{3,2,1,0:T(4,128)} %param.11) | copy-start | bytes 786436
  2.3 0.9 %copy-start.1 = (f32[4,32,4,128]{3,2,1,0:T(4,128)S(1)}, f32[4,32,4,128]{3,2,1,0:T(4,128)}, u32[]{:S(2)}) copy-start(f32[4,32,4,128]{3,2,1,0:T(4,128)} %param.12) | copy-start | bytes 786436
  3.3 0.9 %copy-start.2 = (bf16[1,1,256,256]{3,2,1,0:T(8,128)(2,1)S(1)}, bf16[1,1,256,256]{3,2,1,0:T(8,128)(2,1)}, u32[]{:S(2)}) copy-start(bf16[1,1,256,256]{3,2,1,0:T(8,128)(2,1)} %param.20) | copy-start | bytes 393220
  4.2 0.8 %copy-start.3 = (f32[32,4,128]{2,1,0:T(4,128)S(1)}, f32[32,4,128]{2,1,0:T(4,128)}, u32[]{:S(2)}) copy-start(f32[32,4,128]{2,1,0:T(4,128)} %param.13) | copy-start | bytes 196612
  5.0 0.8 %copy-start.4 = (f32[32,4,128]{2,1,0:T(4,128)S(1)}, f32[32,4,128]{2,1,0:T(4,128)}, u32[]{:S(2)}) copy-start(f32[32,4,128]{2,1,0:T(4,128)} %param.14) | copy-start | bytes 196612
  5.8 0.8 %copy-start.5 = (f32[32,4,128]{2,1,0:T(4,128)S(1)}, f32[32,4,128]{2,1,0:T(4,128)}, u32[]{:S(2)}) copy-start(f32[32,4,128]{2,1,0:T(4,128)} %param.15) | copy-start | bytes 196612
  6.7 0.8 %copy-start.6 = (bf16[1,128,256]{2,1,0:T(8,128)(2,1)S(1)}, bf16[1,128,256]{2,1,0:T(8,128)(2,1)}, u32[]{:S(2)}) copy-start(bf16[1,128,256]{2,1,0:T(8,128)(2,1)} %param.19) | copy-start | bytes 196612
  7.5 0.8 %copy-start.7 = (bf16[1,256,128]{2,1,0:T(8,128)(2,1)S(1)}, bf16[1,256,128]{2,1,0:T(8,128)(2,1)}, u32[]{:S(2)}) copy-start(bf16[1,256,128]{2,1,0:T(8,128)(2,1)} %param.21) | copy-start | bytes 196612

commit v2 on v1

--- a/solution.py
+++ b/solution.py
@@ -171,7 +171,7 @@
 
 
 MESH = pl.DeviceIdType.MESH
-VMEM_BYTES = 48 * 1024 * 1024
+VMEM_BYTES = 61 * 1024 * 1024
 
 
 def matmul(left, right, contract):
@@ -183,9 +183,10 @@
 
 def tile_kernel(
     n_lon, n_lat, n_cl, cap,
+    x_hbm, cot_hbm, diff_hbm, ep_hbm, np_hbm, sea_hbm, dep_hbm, own_hbm, wi_hbm, wm_hbm, wo_hbm,
+    adv_hbm, tend_hbm, sg_hbm, gi_hbm, gm_hbm, go_hbm,
     x_ref, cot_ref, diff_ref, ep_ref, np_ref, sea_ref, dep_ref, own_ref, wi_ref, wm_ref, wo_ref,
-    adv_ref, tend_ref, sg_ref, gi_ref, gm_ref, go_ref,
-    d8, tmp, hal, lat_s, lat_r, lon_s, lon_r, pt, snd, rcv, gis, gms, gos, gir, gmr, gor,
+    adv_ref, tend_ref, sg_ref, gi_ref, gm_ref, go_ref, load_sem, store_sem, d8, tmp, hal, lat_s, lat_r, lon_s, lon_r, pt, snd, rcv, gis, gms, gos, gir, gmr, gor,
     lat_ss, lat_rs, lon_ss, lon_rs, a2a_ss, a2a_rs, g_ss, g_rs,
 ):
     experts = n_lon * n_lat
@@ -205,6 +206,24 @@
     for other in partner_ids[1:] + [east_id, west_id]:
         pl.semaphore_signal(barrier, inc=1, device_id=other, device_id_type=MESH)
 
+    loads = {}
+    for i, (name, src, dst) in enumerate((
+        ("x", x_hbm, x_ref), ("diff", diff_hbm, diff_ref), ("ep", ep_hbm, ep_ref),
+        ("np", np_hbm, np_ref), ("sea", sea_hbm, sea_ref), ("dep", dep_hbm, dep_ref),
+        ("own", own_hbm, own_ref), ("cot", cot_hbm, cot_ref), ("wo", wo_hbm, wo_ref),
+        ("wi", wi_hbm, wi_ref), ("wm", wm_hbm, wm_ref),
+    )):
+        loads[name] = pltpu.make_async_copy(src, dst, load_sem.at[i])
+        loads[name].start()
+
+    results = (
+        (adv_ref, adv_hbm), (tend_ref, tend_hbm), (sg_ref, sg_hbm),
+        (gi_ref, gi_hbm), (gm_ref, gm_hbm), (go_ref, go_hbm),
+    )
+    stores = [
+        pltpu.make_async_copy(a, b, store_sem.at[i]) for i, (a, b) in enumerate(results)
+    ]
+
     rows, wide = x_ref.shape
     tiles = rows // 8
     fields = rows // diff_ref.shape[0]
@@ -217,6 +236,8 @@
     on_tile = lane == tile
     south = jnp.full(cube, lat, jnp.int32) == 0
 
+    for name in ("sea", "dep", "diff", "ep", "np"):
+        loads[name].wait()
     d8[0, 0:4], d8[0, 4:8] = sea_ref[...], sea_ref[...]
     d8[1, 0:4], d8[1, 4:8] = dep_ref[...], dep_ref[...]
     flat = (tiles // fields, 8, wide)
@@ -241,7 +262,7 @@
         pick = jnp.full((feats, wide), lat, jnp.int32) == 0
         lat_s[number] = jnp.where(
             pick, tmp[pl.ds(3, feats, stride=4), :], tmp[pl.ds(0, feats, stride=4), :]
-        )
+        ).astype(jnp.bfloat16)
         lon_s[number, 0] = pack(to_e, wide - 1)
         lon_s[number, 1] = pack(to_w, 0)
         copies = [
@@ -271,8 +292,9 @@
         from_e = jnp.where(
             lane == wide - 1, unpack(lon_r[number, 1]), pltpu.roll(to_w, wide - 1, 2)
         )
-        hal[pl.ds(0, feats, stride=4), :] = lat_r[number]
-        hal[pl.ds(3, feats, stride=4), :] = lat_r[number]
+        beyond = lat_r[number].astype(jnp.float32)
+        hal[pl.ds(0, feats, stride=4), :] = beyond
+        hal[pl.ds(3, feats, stride=4), :] = beyond
         edge = hal[...].reshape(cube)
         from_s = jnp.where(row == 0, jnp.where(south, 0.0, edge), pltpu.roll(to_n, 1, 1))
         from_n = jnp.where(row == 3, jnp.where(south, edge, 0.0), pltpu.roll(to_s, 7, 1))
@@ -313,6 +335,14 @@
             tmp[pl.ds(i, feats, stride=4), :] = columns[:, i * wide : (i + 1) * wide]
         return tmp[...].reshape(four)
 
+    loads["x"].wait()
+    state = x_ref[...].reshape(four)
+    whole = state.reshape(cube)
+    pl.semaphore_wait(barrier, experts - 1 + 2)
+    copies = send_edges(0, whole, whole, whole, whole)
+
+    for name in ("own", "cot"):
+        loads[name].wait()
     count = 4 * wide
     owners = jnp.concatenate([own_ref[i : i + 1, :] for i in range(4)], axis=1)
     hot = (owners == lax.broadcasted_iota(jnp.int32, (experts, count), 0)).astype(jnp.float32)
@@ -330,22 +360,21 @@
     cot = cot_ref[...].reshape(four)
     tmp[...] = (act * cot).reshape(rows, wide)
     to_slots(0, columns_of(tmp))
-
-    pl.semaphore_wait(barrier, experts - 1 + 2)
-
-    state = x_ref[...].reshape(four)
-    sent = []
+    sent = exchange(0)
+
     for number in range(STEPS):
-        whole = state.reshape(cube)
-        copies = send_edges(number, whole, whole, whole, whole)
-        if number == 0:
-            sent = exchange(0)
+        if number > 0:
+            whole = state.reshape(cube)
+            copies = send_edges(number, whole, whole, whole, whole)
         from_w, from_e, from_s, from_n = shifted(number, copies, whole, whole, whole, whole)
         change = c_e * from_e + c_w * from_w + c_n * from_n + c_s * from_s
         state = state + act * (change - c_0 * state)
     adv_ref[...] = state.reshape(rows, wide)
     to_slots(1, columns_of(adv_ref))
     sent_in = exchange(1)
+    stores[0].start()
+    for name in ("wo", "wi", "wm"):
+        loads[name].wait()
     pushed = arrived(0, sent)
     back_2 = matmul(wo_ref[...], pushed, (1, 0))
     inputs = arrived(1, sent_in)
@@ -388,12 +417,29 @@
         from_w, from_e, from_s, from_n = shifted(number, copies, *parts)
         grad = base + from_w + from_e + from_s + from_n
     sg_ref[...] = grad.reshape(rows, wide)
-    tend_ref[...] = (act * to_grid(tend)).reshape(rows, wide)
+    stores[2].start()
+    tend_ref[...] = (act * to_grid(tend)).reshape(rows, wide).astype(jnp.bfloat16)
+    stores[1].start()
     for copy in sent_grads:
         copy.wait()
     gi_ref[...] = gis[...] + gir[...]
     gm_ref[...] = gms[...] + gmr[...]
     go_ref[...] = gos[...] + gor[...]
+    for copy in stores[3:]:
+        copy.start()
+    for copy in stores:
+        copy.wait()
+
+
+def store_kernel(*refs):
+    sem = refs[-1]
+    copies = [
+        pltpu.make_async_copy(refs[i], refs[i + 6], sem.at[i]) for i in range(6)
+    ]
+    for copy in copies:
+        copy.start()
+    for copy in copies:
+        copy.wait()
 
 
 def on_device_fused(
@@ -408,26 +454,31 @@
     cap = 2 * columns // experts
     feats, hidden = w_in.shape[1:]
     f32, bf16 = jnp.float32, jnp.bfloat16
-    vmem = pl.BlockSpec(memory_space=pltpu.VMEM)
+    sizes = [(rows, wide)] * 3 + [(feats, hidden), (hidden, hidden), (hidden, feats)]
+    results = [
+        jax.ShapeDtypeStruct(size, bf16 if i == 1 else f32) for i, size in enumerate(sizes)
+    ]
     flat = lambda v: v.reshape(-1, wide)
+    hbm = pl.BlockSpec(memory_space=pltpu.HBM)
+    operands = (
+        flat(ocean_state), flat(cotangent), flat(diffusivity), flat(east_peclet),
+        flat(north_peclet), sea_mask, depth_levels, flat(owner_table), w_in[0], w_mid[0, 0],
+        w_out[0],
+    )
     out = pl.pallas_call(
         functools.partial(tile_kernel, n_lon, n_lat, n_cl, cap),
-        out_shape=[
-            jax.ShapeDtypeStruct((rows, wide), f32),
-            jax.ShapeDtypeStruct((rows, wide), f32),
-            jax.ShapeDtypeStruct((rows, wide), f32),
-            jax.ShapeDtypeStruct((feats, hidden), f32),
-            jax.ShapeDtypeStruct((hidden, hidden), f32),
-            jax.ShapeDtypeStruct((hidden, feats), f32),
-        ],
-        in_specs=[vmem] * 11,
-        out_specs=[vmem] * 6,
-        scratch_shapes=[
+        out_shape=results,
+        in_specs=[hbm] * 11,
+        out_specs=[hbm] * 6,
+        scratch_shapes=[pltpu.VMEM(v.shape, v.dtype) for v in (*operands, *results)]
+        + [
+            pltpu.SemaphoreType.DMA((11,)),
+            pltpu.SemaphoreType.DMA((6,)),
             pltpu.VMEM((2, 8, wide), jnp.int32),
             pltpu.VMEM((rows, wide), f32),
             pltpu.VMEM((rows, wide), f32),
-            pltpu.VMEM((2 * STEPS, feats, wide), f32),
-            pltpu.VMEM((2 * STEPS, feats, wide), f32),
+            pltpu.VMEM((2 * STEPS, feats, wide), bf16),
+            pltpu.VMEM((2 * STEPS, feats, wide), bf16),
             pltpu.VMEM((2 * STEPS, 2, 8, wide), f32),
             pltpu.VMEM((2 * STEPS, 2, 8, wide), f32),
             pltpu.VMEM((experts * cap, columns), bf16),
@@ -442,15 +493,19 @@
         compiler_params=pltpu.CompilerParams(
             collective_id=0, has_side_effects=True, vmem_limit_bytes=VMEM_BYTES
         ),
-    )(
-        flat(ocean_state), flat(cotangent), flat(diffusivity), flat(east_peclet),
-        flat(north_peclet), sea_mask, depth_levels, flat(owner_table), w_in[0], w_mid[0, 0],
-        w_out[0],
-    )
+    )(*operands)
+    out = pl.pallas_call(
+        store_kernel,
+        out_shape=results,
+        in_specs=[hbm] * 6,
+        out_specs=[hbm] * 6,
+        scratch_shapes=[pltpu.SemaphoreType.DMA((6,))],
+        compiler_params=pltpu.CompilerParams(vmem_limit_bytes=VMEM_BYTES),
+    )(*out)
     advected, tendency, state_grad, grad_in, grad_mid, grad_out = out
     shape = ocean_state.shape
     return (
-        advected.reshape(shape), tendency.astype(bf16).reshape(shape), state_grad.reshape(shape),
+        advected.reshape(shape), tendency.reshape(shape), state_grad.reshape(shape),
         grad_in[None], grad_mid[None, None], grad_out[None],
     )
 

time: 54.4 us -> 78.5 us (1.44)
  Pallas kernels: 41.5 us -> 77.2 us
  local copies, waits for them, and re-layouts: 11.1 us -> 0 us
    pallas_call x0 -> x1, Pallas kernels: none -> 36.9 us  [on_device_fused(): pl.pallas_call(store_kernel, out_shape=results, in_specs=[hbm] * 6, out_s...]
    unnamed x27 -> x0, local copies, waits for them, and re-layouts: 11.1 us -> none
    pallas_call x1, Pallas kernels: 41.5 us -> 40.3 us  [on_device_fused(): pl.pallas_call(functools.partial(tile_kernel, n_lon, n_lat, n_cl, cap), o...]
where the time goes in v2:
time: 78.5 us; the launch traced here: 77.8 us
  Pallas kernels  77.2 us (98%)
    pallas_call x1, Pallas kernels, on_device_fused(): pl.pallas_call(functools.partial(tile_kernel, n_lon, n_lat, n_cl, cap), o...  40.3 us
    pallas_call x1, Pallas kernels, on_device_fused(): pl.pallas_call(store_kernel, out_shape=results, in_specs=[hbm] * 6, out_s...  36.9 us

profile of v2, /device:TPU:1, one launch (start us, length us, event | category | flops | bytes accessed | tf_op | source)
XLA Modules:
  0.0 77.8 jit_solution(6385220781523423439)
XLA Ops:
  0.6 40.3 %shard_map.154 = (f32[512,128]{1,0:T(8,128)}, bf16[512,128]{1,0:T(8,128)(2,1)}, f32[512,128]{1,0:T(8,128)}, f32[128,256]{1,0:T(8,128)}, f32[256,256]{1,0:T(8,128)}, /*index=5*/f32[256,128]{1,0:T(8,128)}) custom-call(f32[512,128]{1,0:T(8,128)} %bitcast.15, f32[512,128]{1,0:T(8,128)} %bitcast.16, f32[128,128]{1,0:T(8,128)} %bitcast.18, f32[128,128]{1,0:T(8,128)} %bitcast.19, ...), custom_call_target="tpu_custom_call" | custom-call | tf_op jit(solution)/shard_map/pallas_call | solution.py:468
  40.9 36.9 %shard_map.155 = (f32[512,128]{1,0:T(8,128)}, bf16[512,128]{1,0:T(8,128)(2,1)}, f32[512,128]{1,0:T(8,128)}, f32[128,256]{1,0:T(8,128)}, f32[256,256]{1,0:T(8,128)}, /*index=5*/f32[256,128]{1,0:T(8,128)}) custom-call(f32[512,128]{1,0:T(8,128)} %get-tuple-element.18.refs_0_, bf16[512,128]{1,0:T(8,128)(2,1)} %get-tuple-element.19.refs_1_, ...), custom_call_target="tpu_custom_call" | custom-call | tf_op jit(solution)/shard_map/pallas_call | solution.py:497

commit v3 on v2

--- a/solution.py
+++ b/solution.py
@@ -393,7 +393,6 @@
     raw = matmul(wo_ref[...], a_1, (0, 0)).astype(jnp.bfloat16)
     for e in range(experts):
         snd[3, e] = raw[:, e * cap : (e + 1) * cap]
-    sent_raw = exchange(3)
     gis[...] = matmul(inputs, delta_0, (1, 1))
     gms[...] = matmul(a_0, delta_1, (1, 1))
     gos[...] = matmul(a_1, pushed, (1, 1))
@@ -411,6 +410,8 @@
         held = act * grad
         parts = [(c * held).reshape(cube) for c in (c_e, c_w, c_n, c_s)]
         copies = send_edges(number, *parts)
+        if number == STEPS:
+            sent_raw = exchange(3)
         base = grad - c_0 * held
         if number == 2 * STEPS - 1:
             tend = arrived(3, sent_raw)
@@ -432,13 +433,15 @@
 
 
 def store_kernel(*refs):
-    sem = refs[-1]
-    copies = [
-        pltpu.make_async_copy(refs[i], refs[i + 6], sem.at[i]) for i in range(6)
-    ]
-    for copy in copies:
+    sems = refs[-1]
+    loads = [pltpu.make_async_copy(refs[i], refs[i + 12], sems.at[0, i]) for i in range(6)]
+    stores = [pltpu.make_async_copy(refs[i + 12], refs[i + 6], sems.at[1, i]) for i in range(6)]
+    for copy in loads:
         copy.start()
-    for copy in copies:
+    for load, store in zip(loads, stores):
+        load.wait()
+        store.start()
+    for copy in stores:
         copy.wait()
 
 
@@ -499,7 +502,8 @@
         out_shape=results,
         in_specs=[hbm] * 6,
         out_specs=[hbm] * 6,
-        scratch_shapes=[pltpu.SemaphoreType.DMA((6,))],
+        scratch_shapes=[pltpu.VMEM(v.shape, v.dtype) for v in results]
+        + [pltpu.SemaphoreType.DMA((2, 6))],
         compiler_params=pltpu.CompilerParams(vmem_limit_bytes=VMEM_BYTES),
     )(*out)
     advected, tendency, state_grad, grad_in, grad_mid, grad_out = out

time: 78.5 us -> 41.3 us (0.53)
  Pallas kernels: 77.2 us -> 40.4 us
    pallas_call x1, Pallas kernels: 36.9 us -> 2.07 us  [on_device_fused(): pl.pallas_call(store_kernel, out_shape=results, in_specs=[hbm] * 6, out_s...]
    pallas_call x1, Pallas kernels: 40.3 us -> 38.3 us  [on_device_fused(): pl.pallas_call(functools.partial(tile_kernel, n_lon, n_lat, n_cl, cap), o...]
where the time goes in v3:
time: 41.3 us; the launch traced here: 41.1 us
  Pallas kernels  40.4 us (98%)
  between operations  0.64 us (2%)
    pallas_call x1, Pallas kernels, on_device_fused(): pl.pallas_call(functools.partial(tile_kernel, n_lon, n_lat, n_cl, cap), o...  38.3 us
    pallas_call x1, Pallas kernels, on_device_fused(): pl.pallas_call(store_kernel, out_shape=results, in_specs=[hbm] * 6, out_s...  2.07 us

profile of v3, /device:TPU:1, one launch (start us, length us, event | category | flops | bytes accessed | tf_op | source)
XLA Modules:
  0.0 41.1 jit_solution(13535049176009367164)
XLA Ops:
  0.6 38.3 %shard_map.154 = (f32[512,128]{1,0:T(8,128)}, bf16[512,128]{1,0:T(8,128)(2,1)}, f32[512,128]{1,0:T(8,128)}, f32[128,256]{1,0:T(8,128)}, f32[256,256]{1,0:T(8,128)}, /*index=5*/f32[256,128]{1,0:T(8,128)}) custom-call(f32[512,128]{1,0:T(8,128)} %bitcast.15, f32[512,128]{1,0:T(8,128)} %bitcast.16, f32[128,128]{1,0:T(8,128)} %bitcast.18, f32[128,128]{1,0:T(8,128)} %bitcast.19, ...), custom_call_target="tpu_custom_call" | custom-call | tf_op jit(solution)/shard_map/pallas_call | solution.py:471
  39.0 2.1 %shard_map.155 = (f32[512,128]{1,0:T(8,128)}, bf16[512,128]{1,0:T(8,128)(2,1)}, f32[512,128]{1,0:T(8,128)}, f32[128,256]{1,0:T(8,128)}, f32[256,256]{1,0:T(8,128)}, /*index=5*/f32[256,128]{1,0:T(8,128)}) custom-call(f32[512,128]{1,0:T(8,128)} %get-tuple-element.18.refs_0_, bf16[512,128]{1,0:T(8,128)(2,1)} %get-tuple-element.19.refs_1_, ...), custom_call_target="tpu_custom_call" | custom-call | tf_op jit(solution)/shard_map/pallas_call | solution.py:500

commit v4 on v3

--- a/solution.py
+++ b/solution.py
@@ -186,8 +186,11 @@
     x_hbm, cot_hbm, diff_hbm, ep_hbm, np_hbm, sea_hbm, dep_hbm, own_hbm, wi_hbm, wm_hbm, wo_hbm,
     adv_hbm, tend_hbm, sg_hbm, gi_hbm, gm_hbm, go_hbm,
     x_ref, cot_ref, diff_ref, ep_ref, np_ref, sea_ref, dep_ref, own_ref, wi_ref, wm_ref, wo_ref,
-    adv_ref, tend_ref, sg_ref, gi_ref, gm_ref, go_ref, load_sem, store_sem, d8, tmp, hal, lat_s, lat_r, lon_s, lon_r, pt, snd, rcv, gis, gms, gos, gir, gmr, gor,
-    lat_ss, lat_rs, lon_ss, lon_rs, a2a_ss, a2a_rs, g_ss, g_rs,
+    adv_ref, tend_ref, sg_ref, gi_ref, gm_ref, go_ref, load_sem, store_sem, d8, tmp, hal, lat_s, lat_r, lon_s, lon_r, pt, snd, rcv,
+    wi_far, wm_far, wo_far, gi_own, gm_own, go_own, gi_far, gm_far, go_far,
+    gi_one, gm_one, go_one, gi_two, gm_two, go_two,
+    gi_out, gm_out, go_out, gi_got, gm_got, go_got,
+    lat_ss, lat_rs, lon_ss, lon_rs, a2a_ss, a2a_rs, w_ss, w_rs, g_ss, g_rs,
 ):
     experts = n_lon * n_lat
     lon, lat, cl = lax.axis_index("lon"), lax.axis_index("lat"), lax.axis_index("cl")
@@ -198,12 +201,16 @@
     west_id = {"lon": west // n_cl, "cl": west % n_cl}
     lat_id = {"lat": 1 - lat}
     cl_id = {"cl": 1 - cl}
-    me = lon * n_lat + lat
-    partners = [(me + d) % experts for d in range(experts)]
-    partner_ids = [{"lon": p // n_lat, "lat": p % n_lat} for p in partners]
+    deep = n_lon // 2
+    members = deep * n_lat
+    half = lon // deep
+    me = (lon % deep) * n_lat + lat
+    partners = [(me + d) % members for d in range(members)]
+    partner_ids = [{"lon": half * deep + p // n_lat, "lat": p % n_lat} for p in partners]
+    far_id = {"lon": (lon + deep) % n_lon}
 
     barrier = pltpu.get_barrier_semaphore()
-    for other in partner_ids[1:] + [east_id, west_id]:
+    for other in partner_ids[1:] + [east_id, west_id, far_id]:
         pl.semaphore_signal(barrier, inc=1, device_id=other, device_id_type=MESH)
 
     loads = {}
@@ -302,7 +309,7 @@
 
     def exchange(kind):
         copies = []
-        for d in range(1, experts):
+        for d in range(1, members):
             copies.append(
                 pltpu.make_async_remote_copy(
                     snd.at[kind, partners[d]], rcv.at[kind, me],
@@ -314,10 +321,37 @@
         rcv[kind, me] = snd[kind, me]
         return copies
 
-    def arrived(kind, copies):
+    def gathered(kind, side):
+        return jnp.concatenate([rcv[kind, q, side] for q in range(members)], axis=1)
+
+    def returned(kind, copies):
         for copy in copies:
             copy.wait()
-        return jnp.concatenate([rcv[kind, e] for e in range(experts)], axis=1)
+        return jnp.concatenate(
+            [rcv[kind, e % members, e // members] for e in range(experts)], axis=1
+        )
+
+    def keep(kind, side, slots):
+        for q in range(members):
+            snd[kind, q, side] = slots[:, q * cap : (q + 1) * cap]
+
+    def halves(refs, which):
+        return [
+            ref.at[pl.ds(pl.multiple_of(which * (ref.shape[0] // 2), 64), ref.shape[0] // 2), :]
+            for ref in refs
+        ]
+
+    def send_all(sources, targets, ss, rs, number, where):
+        copies = [
+            pltpu.make_async_remote_copy(
+                src, dst, ss.at[number, i], rs.at[number, i],
+                device_id=where, device_id_type=MESH,
+            )
+            for i, (src, dst) in enumerate(zip(sources, targets))
+        ]
+        for copy in copies:
+            copy.start()
+        return copies
 
     def columns_of(ref):
         return jnp.concatenate(
@@ -327,7 +361,7 @@
     def to_slots(kind, columns):
         slots = matmul(columns, pt[...], (1, 1)).astype(jnp.bfloat16)
         for e in range(experts):
-            snd[kind, e] = slots[:, e * cap : (e + 1) * cap]
+            snd[kind, e % members, e // members] = slots[:, e * cap : (e + 1) * cap]
 
     def to_grid(slots):
         columns = matmul(slots, pt[...], (1, 0))
@@ -338,8 +372,14 @@
     loads["x"].wait()
     state = x_ref[...].reshape(four)
     whole = state.reshape(cube)
-    pl.semaphore_wait(barrier, experts - 1 + 2)
+    pl.semaphore_wait(barrier, members - 1 + 3)
     copies = send_edges(0, whole, whole, whole, whole)
+    for name in ("wo", "wi", "wm"):
+        loads[name].wait()
+    weights, far_weights = (wi_ref, wm_ref, wo_ref), (wi_far, wm_far, wo_far)
+    sent_far = send_all(
+        halves(weights, cl), halves(far_weights, cl), w_ss, w_rs, 0, far_id
+    )
 
     for name in ("own", "cot"):
         loads[name].wait()
@@ -373,39 +413,48 @@
     to_slots(1, columns_of(adv_ref))
     sent_in = exchange(1)
     stores[0].start()
-    for name in ("wo", "wi", "wm"):
-        loads[name].wait()
-    pushed = arrived(0, sent)
-    back_2 = matmul(wo_ref[...], pushed, (1, 0))
-    inputs = arrived(1, sent_in)
-
-    t_0 = jnp.tanh(matmul(wi_ref[...], inputs, (0, 0)))
-    a_0 = t_0.astype(jnp.bfloat16)
-    t_1 = jnp.tanh(matmul(wm_ref[...], a_0, (0, 0)))
-    a_1 = t_1.astype(jnp.bfloat16)
-    delta_1 = (back_2 * (1.0 - t_1 * t_1)).astype(jnp.bfloat16)
-    back_1 = matmul(wm_ref[...], delta_1, (1, 0))
-    delta_0 = (back_1 * (1.0 - t_0 * t_0)).astype(jnp.bfloat16)
-    back_in = matmul(wi_ref[...], delta_0, (1, 0)).astype(jnp.bfloat16)
-    for e in range(experts):
-        snd[2, e] = back_in[:, e * cap : (e + 1) * cap]
+    for copy in sent_far:
+        copy.wait()
+    sent_near = send_all(
+        halves(far_weights, cl), halves(far_weights, cl), w_ss, w_rs, 1, cl_id
+    )
+    for copy in sent + sent_near + sent_in:
+        copy.wait()
+
+    sides = (1 - half, half)
+    sets = (far_weights, weights)
+    pushed = [gathered(0, side) for side in sides]
+    inputs = [gathered(1, side) for side in sides]
+    t_0 = [jnp.tanh(matmul(w[0][...], v, (0, 0))) for w, v in zip(sets, inputs)]
+    a_0 = [t.astype(jnp.bfloat16) for t in t_0]
+    back_2 = [matmul(w[2][...], v, (1, 0)) for w, v in zip(sets, pushed)]
+    t_1 = [jnp.tanh(matmul(w[1][...], a, (0, 0))) for w, a in zip(sets, a_0)]
+    a_1 = [t.astype(jnp.bfloat16) for t in t_1]
+    delta_1 = [(b * (1.0 - t * t)).astype(jnp.bfloat16) for b, t in zip(back_2, t_1)]
+    back_1 = [matmul(w[1][...], d, (1, 0)) for w, d in zip(sets, delta_1)]
+    delta_0 = [(b * (1.0 - t * t)).astype(jnp.bfloat16) for b, t in zip(back_1, t_0)]
+    for side, w, d in zip(sides, sets, delta_0):
+        keep(2, side, matmul(w[0][...], d, (1, 0)).astype(jnp.bfloat16))
     sent_back = exchange(2)
-    raw = matmul(wo_ref[...], a_1, (0, 0)).astype(jnp.bfloat16)
-    for e in range(experts):
-        snd[3, e] = raw[:, e * cap : (e + 1) * cap]
-    gis[...] = matmul(inputs, delta_0, (1, 1))
-    gms[...] = matmul(a_0, delta_1, (1, 1))
-    gos[...] = matmul(a_1, pushed, (1, 1))
-    sent_grads = []
-    for i, (src, dst) in enumerate(((gis, gir), (gms, gmr), (gos, gor))):
-        sent_grads.append(
-            pltpu.make_async_remote_copy(
-                src, dst, g_ss.at[i], g_rs.at[i], device_id=cl_id, device_id_type=MESH
-            )
-        )
-        sent_grads[-1].start()
-
-    grad = cot + to_grid(arrived(2, sent_back))
+    own, far = (gi_own, gm_own, go_own), (gi_far, gm_far, go_far)
+    one, two = (gi_one, gm_one, go_one), (gi_two, gm_two, go_two)
+    out, got = (gi_out, gm_out, go_out), (gi_got, gm_got, go_got)
+    sums = (gi_ref, gm_ref, go_ref)
+    sent_sums = []
+    for i, (partial, landing) in enumerate(((far, two), (own, one))):
+        partial[0][...] = matmul(inputs[i], delta_0[i], (1, 1))
+        partial[1][...] = matmul(a_0[i], delta_1[i], (1, 1))
+        partial[2][...] = matmul(a_1[i], pushed[i], (1, 1))
+        sent_sums.append(send_all(halves(partial, 1 - cl), landing, g_ss, g_rs, i, cl_id))
+    for side, w, a in zip(sides, sets, a_1):
+        keep(3, side, matmul(w[2][...], a, (0, 0)).astype(jnp.bfloat16))
+    for copy in sent_sums[0]:
+        copy.wait()
+    for target, mine, other in zip(out, halves(far, cl), two):
+        target[...] = (mine[...] + other[...]).astype(jnp.bfloat16)
+    sent_out = send_all(out, got, g_ss, g_rs, 2, far_id)
+
+    grad = cot + to_grid(returned(2, sent_back))
     for number in range(STEPS, 2 * STEPS):
         held = act * grad
         parts = [(c * held).reshape(cube) for c in (c_e, c_w, c_n, c_s)]
@@ -414,18 +463,19 @@
             sent_raw = exchange(3)
         base = grad - c_0 * held
         if number == 2 * STEPS - 1:
-            tend = arrived(3, sent_raw)
+            tend = returned(3, sent_raw)
         from_w, from_e, from_s, from_n = shifted(number, copies, *parts)
         grad = base + from_w + from_e + from_s + from_n
     sg_ref[...] = grad.reshape(rows, wide)
     stores[2].start()
     tend_ref[...] = (act * to_grid(tend)).reshape(rows, wide).astype(jnp.bfloat16)
     stores[1].start()
-    for copy in sent_grads:
-        copy.wait()
-    gi_ref[...] = gis[...] + gir[...]
-    gm_ref[...] = gms[...] + gmr[...]
-    go_ref[...] = gos[...] + gor[...]
+    for copy in sent_sums[1] + sent_out:
+        copy.wait()
+    for target, mine, a, b in zip(halves(sums, cl), halves(own, cl), one, got):
+        target[...] = mine[...] + a[...] + b[...].astype(jnp.float32)
+    for copy in send_all(halves(sums, cl), halves(sums, cl), g_ss, g_rs, 3, cl_id):
+        copy.wait()
     for copy in stores[3:]:
         copy.start()
     for copy in stores:
@@ -485,14 +535,18 @@
             pltpu.VMEM((2 * STEPS, 2, 8, wide), f32),
             pltpu.VMEM((2 * STEPS, 2, 8, wide), f32),
             pltpu.VMEM((experts * cap, columns), bf16),
-            pltpu.VMEM((4, experts, feats, cap), bf16),
-            pltpu.VMEM((4, experts, feats, cap), bf16),
+            pltpu.VMEM((4, experts // 2, 2, feats, cap), bf16),
+            pltpu.VMEM((4, experts // 2, 2, feats, cap), bf16),
         ]
-        + [pltpu.VMEM(s, f32) for s in ((feats, hidden), (hidden, hidden), (hidden, feats))] * 2
+        + [pltpu.VMEM(size, bf16) for size in sizes[3:]]
+        + [pltpu.VMEM(size, f32) for size in sizes[3:]] * 2
+        + [pltpu.VMEM((size[0] // 2, size[1]), f32) for size in sizes[3:]] * 2
+        + [pltpu.VMEM((size[0] // 2, size[1]), bf16) for size in sizes[3:]] * 2
         + [pltpu.SemaphoreType.DMA((2 * STEPS,))] * 2
         + [pltpu.SemaphoreType.DMA((2 * STEPS, 2))] * 2
-        + [pltpu.SemaphoreType.DMA((4, experts))] * 2
-        + [pltpu.SemaphoreType.DMA((3,))] * 2,
+        + [pltpu.SemaphoreType.DMA((4, experts // 2))] * 2
+        + [pltpu.SemaphoreType.DMA((2, 3))] * 2
+        + [pltpu.SemaphoreType.DMA((4, 3))] * 2,
         compiler_params=pltpu.CompilerParams(
             collective_id=0, has_side_effects=True, vmem_limit_bytes=VMEM_BYTES
         ),
@@ -515,7 +569,7 @@
 
 
 def solution(mesh):
-    few = mesh.shape["lat"] == 2 and mesh.shape["cl"] == 2 and 2 < mesh.shape["lon"] <= 4
+    few = mesh.shape["lat"] == 2 and mesh.shape["cl"] == 2 and mesh.shape["lon"] == 4
     plan = on_device_fused if few else on_device
     return jax.shard_map(
         plan,

time: 41.3 us -> 37.9 us (0.918)
  Pallas kernels: 40.4 us -> 37.1 us
    pallas_call x1, Pallas kernels: 38.3 us -> 35 us  [on_device_fused(): pl.pallas_call(functools.partial(tile_kernel, n_lon, n_lat, n_cl, cap), o...]
where the time goes in v4:
time: 37.9 us; the launch traced here: 37.7 us
  Pallas kernels  37.1 us (98%)
  between operations  0.64 us (2%)
    pallas_call x1, Pallas kernels, on_device_fused(): pl.pallas_call(functools.partial(tile_kernel, n_lon, n_lat, n_cl, cap), o...  35 us
    pallas_call x1, Pallas kernels, on_device_fused(): pl.pallas_call(store_kernel, out_shape=results, in_specs=[hbm] * 6, out_s...  2.07 us

profile of v4, /device:TPU:1, one launch (start us, length us, event | category | flops | bytes accessed | tf_op | source)
XLA Modules:
  0.0 37.7 jit_solution(2237079398249034960)
XLA Ops:
  0.6 35.0 %shard_map.154 = (f32[512,128]{1,0:T(8,128)}, bf16[512,128]{1,0:T(8,128)(2,1)}, f32[512,128]{1,0:T(8,128)}, f32[128,256]{1,0:T(8,128)}, f32[256,256]{1,0:T(8,128)}, /*index=5*/f32[256,128]{1,0:T(8,128)}) custom-call(f32[512,128]{1,0:T(8,128)} %bitcast.15, f32[512,128]{1,0:T(8,128)} %bitcast.16, f32[128,128]{1,0:T(8,128)} %bitcast.18, f32[128,128]{1,0:T(8,128)} %bitcast.19, ...), custom_call_target="tpu_custom_call" | custom-call | tf_op jit(solution)/shard_map/pallas_call | solution.py:521
  35.6 2.1 %shard_map.155 = (f32[512,128]{1,0:T(8,128)}, bf16[512,128]{1,0:T(8,128)(2,1)}, f32[512,128]{1,0:T(8,128)}, f32[128,256]{1,0:T(8,128)}, f32[256,256]{1,0:T(8,128)}, /*index=5*/f32[256,128]{1,0:T(8,128)}) custom-call(f32[512,128]{1,0:T(8,128)} %get-tuple-element.18.refs_0_, bf16[512,128]{1,0:T(8,128)(2,1)} %get-tuple-element.19.refs_1_, ...), custom_call_target="tpu_custom_call" | custom-call | tf_op jit(solution)/shard_map/pallas_call | solution.py:554

commit v5 on v4

--- a/solution.py
+++ b/solution.py
@@ -215,9 +215,9 @@
 
     loads = {}
     for i, (name, src, dst) in enumerate((
-        ("x", x_hbm, x_ref), ("diff", diff_hbm, diff_ref), ("ep", ep_hbm, ep_ref),
+        ("own", own_hbm, own_ref), ("x", x_hbm, x_ref), ("diff", diff_hbm, diff_ref), ("ep", ep_hbm, ep_ref),
         ("np", np_hbm, np_ref), ("sea", sea_hbm, sea_ref), ("dep", dep_hbm, dep_ref),
-        ("own", own_hbm, own_ref), ("cot", cot_hbm, cot_ref), ("wo", wo_hbm, wo_ref),
+        ("cot", cot_hbm, cot_ref), ("wo", wo_hbm, wo_ref),
         ("wi", wi_hbm, wi_ref), ("wm", wm_hbm, wm_ref),
     )):
         loads[name] = pltpu.make_async_copy(src, dst, load_sem.at[i])
@@ -257,6 +257,18 @@
     c_e, c_w = (diff * (1.0 - ep))[None], (diff * (1.0 + ep))[None]
     c_n, c_s = (diff * (1.0 - np_))[None], (diff * (1.0 + np_))[None]
     c_0, act = (4.0 * diff)[None], active[None]
+    flat_lane = lax.broadcasted_iota(jnp.int32, flat, 2)
+    flat_row = lax.broadcasted_iota(jnp.int32, flat, 1) % 4
+    flat_south = jnp.full(flat, lat, jnp.int32) == 0
+    a_e, a_w, a_n, a_s = act * c_e, act * c_w, act * c_n, act * c_s
+    a_c = act * c_0
+    rim_e = jnp.where(flat_lane == wide - 1, a_e[0], 0.0)[None]
+    rim_w = jnp.where(flat_lane == 0, a_w[0], 0.0)[None]
+    rim_lat = jnp.where(
+        flat_south,
+        jnp.where(flat_row == 3, a_n[0], 0.0),
+        jnp.where(flat_row == 0, a_s[0], 0.0),
+    )[None]
 
     def pack(value, side):
         return jnp.sum(jnp.where(on_tile, value[:, :, side : side + 1], 0.0), axis=0)
@@ -264,7 +276,7 @@
     def unpack(packed):
         return jnp.sum(jnp.where(on_tile, packed[None], 0.0), axis=2, keepdims=True)
 
-    def send_edges(number, to_e, to_w, to_n, to_s):
+    def fill_edges(number, to_e, to_w, to_n, to_s):
         tmp[...] = jnp.where(south, to_n, to_s).reshape(rows, wide)
         pick = jnp.full((feats, wide), lat, jnp.int32) == 0
         lat_s[number] = jnp.where(
@@ -272,6 +284,8 @@
         ).astype(jnp.bfloat16)
         lon_s[number, 0] = pack(to_e, wide - 1)
         lon_s[number, 1] = pack(to_w, 0)
+
+    def start_edges(number):
         copies = [
             pltpu.make_async_remote_copy(
                 lat_s.at[number], lat_r.at[number], lat_ss.at[number], lat_rs.at[number],
@@ -292,20 +306,24 @@
             copy.start()
         return copies
 
-    def shifted(number, copies, to_e, to_w, to_n, to_s):
+    def inside(to_e, to_w, to_n, to_s):
+        from_w = jnp.where(lane == 0, 0.0, pltpu.roll(to_e, 1, 2))
+        from_e = jnp.where(lane == wide - 1, 0.0, pltpu.roll(to_w, wide - 1, 2))
+        from_s = jnp.where(row == 0, 0.0, pltpu.roll(to_n, 1, 1))
+        from_n = jnp.where(row == 3, 0.0, pltpu.roll(to_s, 7, 1))
+        return [v.reshape(four) for v in (from_w, from_e, from_s, from_n)]
+
+    def outside(number, copies):
         for copy in copies:
             copy.wait()
-        from_w = jnp.where(lane == 0, unpack(lon_r[number, 0]), pltpu.roll(to_e, 1, 2))
-        from_e = jnp.where(
-            lane == wide - 1, unpack(lon_r[number, 1]), pltpu.roll(to_w, wide - 1, 2)
-        )
         beyond = lat_r[number].astype(jnp.float32)
         hal[pl.ds(0, feats, stride=4), :] = beyond
         hal[pl.ds(3, feats, stride=4), :] = beyond
-        edge = hal[...].reshape(cube)
-        from_s = jnp.where(row == 0, jnp.where(south, 0.0, edge), pltpu.roll(to_n, 1, 1))
-        from_n = jnp.where(row == 3, jnp.where(south, edge, 0.0), pltpu.roll(to_s, 7, 1))
-        return [v.reshape(four) for v in (from_w, from_e, from_s, from_n)]
+        return (
+            unpack(lon_r[number, 0]).reshape((*four[:3], 1)),
+            unpack(lon_r[number, 1]).reshape((*four[:3], 1)),
+            hal[...].reshape(four),
+        )
 
     def exchange(kind):
         copies = []
@@ -369,20 +387,7 @@
             tmp[pl.ds(i, feats, stride=4), :] = columns[:, i * wide : (i + 1) * wide]
         return tmp[...].reshape(four)
 
-    loads["x"].wait()
-    state = x_ref[...].reshape(four)
-    whole = state.reshape(cube)
-    pl.semaphore_wait(barrier, members - 1 + 3)
-    copies = send_edges(0, whole, whole, whole, whole)
-    for name in ("wo", "wi", "wm"):
-        loads[name].wait()
-    weights, far_weights = (wi_ref, wm_ref, wo_ref), (wi_far, wm_far, wo_far)
-    sent_far = send_all(
-        halves(weights, cl), halves(far_weights, cl), w_ss, w_rs, 0, far_id
-    )
-
-    for name in ("own", "cot"):
-        loads[name].wait()
+    loads["own"].wait()
     count = 4 * wide
     owners = jnp.concatenate([own_ref[i : i + 1, :] for i in range(4)], axis=1)
     hot = (owners == lax.broadcasted_iota(jnp.int32, (experts, count), 0)).astype(jnp.float32)
@@ -397,6 +402,21 @@
         lax.broadcasted_iota(jnp.int32, (experts * cap, count), 0) == slot
     ).astype(jnp.float32).astype(jnp.bfloat16)
 
+    loads["x"].wait()
+    state = x_ref[...].reshape(four)
+    whole = state.reshape(cube)
+    hal[...] = jnp.zeros_like(hal)
+    fill_edges(0, whole, whole, whole, whole)
+    pl.semaphore_wait(barrier, members - 1 + 3)
+    copies = start_edges(0)
+    for name in ("wo", "wi", "wm"):
+        loads[name].wait()
+    weights, far_weights = (wi_ref, wm_ref, wo_ref), (wi_far, wm_far, wo_far)
+    sent_far = send_all(
+        halves(weights, cl), halves(far_weights, cl), w_ss, w_rs, 0, far_id
+    )
+
+    loads["cot"].wait()
     cot = cot_ref[...].reshape(four)
     tmp[...] = (act * cot).reshape(rows, wide)
     to_slots(0, columns_of(tmp))
@@ -405,10 +425,14 @@
     for number in range(STEPS):
         if number > 0:
             whole = state.reshape(cube)
-            copies = send_edges(number, whole, whole, whole, whole)
-        from_w, from_e, from_s, from_n = shifted(number, copies, whole, whole, whole, whole)
-        change = c_e * from_e + c_w * from_w + c_n * from_n + c_s * from_s
-        state = state + act * (change - c_0 * state)
+            fill_edges(number, whole, whole, whole, whole)
+            copies = start_edges(number)
+        from_w, from_e, from_s, from_n = inside(whole, whole, whole, whole)
+        state = state - a_c * state + (
+            a_e * from_e + a_w * from_w + a_n * from_n + a_s * from_s
+        )
+        out_w, out_e, out_lat = outside(number, copies)
+        state = state + (rim_w * out_w + rim_e * out_e + rim_lat * out_lat)
     adv_ref[...] = state.reshape(rows, wide)
     to_slots(1, columns_of(adv_ref))
     sent_in = exchange(1)
@@ -454,27 +478,36 @@
         target[...] = (mine[...] + other[...]).astype(jnp.bfloat16)
     sent_out = send_all(out, got, g_ss, g_rs, 2, far_id)
 
+    four_lane = lane.reshape(four)
+    four_rim = jnp.where(south, row, 3 - row).reshape(four) == 3
     grad = cot + to_grid(returned(2, sent_back))
     for number in range(STEPS, 2 * STEPS):
         held = act * grad
         parts = [(c * held).reshape(cube) for c in (c_e, c_w, c_n, c_s)]
-        copies = send_edges(number, *parts)
+        fill_edges(number, *parts)
+        copies = start_edges(number)
         if number == STEPS:
             sent_raw = exchange(3)
-        base = grad - c_0 * held
-        if number == 2 * STEPS - 1:
-            tend = returned(3, sent_raw)
-        from_w, from_e, from_s, from_n = shifted(number, copies, *parts)
-        grad = base + from_w + from_e + from_s + from_n
+        grad = grad - c_0 * held
+        for part in inside(*parts):
+            grad = grad + part
+        out_w, out_e, out_lat = outside(number, copies)
+        grad = grad + (
+            jnp.where(four_lane == 0, out_w, 0.0)
+            + jnp.where(four_lane == wide - 1, out_e, 0.0)
+            + jnp.where(four_rim, out_lat, 0.0)
+        )
     sg_ref[...] = grad.reshape(rows, wide)
     stores[2].start()
-    tend_ref[...] = (act * to_grid(tend)).reshape(rows, wide).astype(jnp.bfloat16)
-    stores[1].start()
     for copy in sent_sums[1] + sent_out:
         copy.wait()
     for target, mine, a, b in zip(halves(sums, cl), halves(own, cl), one, got):
         target[...] = mine[...] + a[...] + b[...].astype(jnp.float32)
-    for copy in send_all(halves(sums, cl), halves(sums, cl), g_ss, g_rs, 3, cl_id):
+    sent_last = send_all(halves(sums, cl), halves(sums, cl), g_ss, g_rs, 3, cl_id)
+    tend = returned(3, sent_raw)
+    tend_ref[...] = (act * to_grid(tend)).reshape(rows, wide).astype(jnp.bfloat16)
+    stores[1].start()
+    for copy in sent_last:
         copy.wait()
     for copy in stores[3:]:
         copy.start()

time: 37.9 us -> 37.7 us (level)
  no operation moved by 1% of the time
where the time goes in v5:
time: 37.7 us; the launch traced here: 37.5 us
  Pallas kernels  36.8 us (98%)
  between operations  0.64 us (2%)
    pallas_call x1, Pallas kernels, on_device_fused(): pl.pallas_call(functools.partial(tile_kernel, n_lon, n_lat, n_cl, cap), o...  34.8 us
    pallas_call x1, Pallas kernels, on_device_fused(): pl.pallas_call(store_kernel, out_shape=results, in_specs=[hbm] * 6, out_s...  2.07 us

profile of v5, /device:TPU:1, one launch (start us, length us, event | category | flops | bytes accessed | tf_op | source)
XLA Modules:
  0.0 37.5 jit_solution(3515305765339260061)
XLA Ops:
  0.6 34.8 %shard_map.154 = (f32[512,128]{1,0:T(8,128)}, bf16[512,128]{1,0:T(8,128)(2,1)}, f32[512,128]{1,0:T(8,128)}, f32[128,256]{1,0:T(8,128)}, f32[256,256]{1,0:T(8,128)}, /*index=5*/f32[256,128]{1,0:T(8,128)}) custom-call(f32[512,128]{1,0:T(8,128)} %bitcast.15, f32[512,128]{1,0:T(8,128)} %bitcast.16, f32[128,128]{1,0:T(8,128)} %bitcast.18, f32[128,128]{1,0:T(8,128)} %bitcast.19, ...), custom_call_target="tpu_custom_call" | custom-call | tf_op jit(solution)/shard_map/pallas_call | solution.py:554
  35.4 2.1 %shard_map.155 = (f32[512,128]{1,0:T(8,128)}, bf16[512,128]{1,0:T(8,128)(2,1)}, f32[512,128]{1,0:T(8,128)}, f32[128,256]{1,0:T(8,128)}, f32[256,256]{1,0:T(8,128)}, /*index=5*/f32[256,128]{1,0:T(8,128)}) custom-call(f32[512,128]{1,0:T(8,128)} %get-tuple-element.18.refs_0_, bf16[512,128]{1,0:T(8,128)(2,1)} %get-tuple-element.19.refs_1_, ...), custom_call_target="tpu_custom_call" | custom-call | tf_op jit(solution)/shard_map/pallas_call | solution.py:587

commit v6 on v5

--- a/solution.py
+++ b/solution.py
@@ -412,9 +412,6 @@
     for name in ("wo", "wi", "wm"):
         loads[name].wait()
     weights, far_weights = (wi_ref, wm_ref, wo_ref), (wi_far, wm_far, wo_far)
-    sent_far = send_all(
-        halves(weights, cl), halves(far_weights, cl), w_ss, w_rs, 0, far_id
-    )
 
     loads["cot"].wait()
     cot = cot_ref[...].reshape(four)
@@ -427,6 +424,10 @@
             whole = state.reshape(cube)
             fill_edges(number, whole, whole, whole, whole)
             copies = start_edges(number)
+        if number == STEPS - 1:
+            sent_far = send_all(
+                halves(weights, cl), halves(far_weights, cl), w_ss, w_rs, 0, far_id
+            )
         from_w, from_e, from_s, from_n = inside(whole, whole, whole, whole)
         state = state - a_c * state + (
             a_e * from_e + a_w * from_w + a_n * from_n + a_s * from_s

time: 37.7 us -> 39.2 us (1.040)
  Pallas kernels: 36.8 us -> 38.3 us
    pallas_call x1, Pallas kernels: 34.8 us -> 36.2 us  [on_device_fused(): pl.pallas_call(functools.partial(tile_kernel, n_lon, n_lat, n_cl, cap), o...]
where the time goes in v6:
time: 39.2 us; the launch traced here: 38.9 us
  Pallas kernels  38.3 us (98%)
  between operations  0.64 us (2%)
    pallas_call x1, Pallas kernels, on_device_fused(): pl.pallas_call(functools.partial(tile_kernel, n_lon, n_lat, n_cl, cap), o...  36.2 us
    pallas_call x1, Pallas kernels, on_device_fused(): pl.pallas_call(store_kernel, out_shape=results, in_specs=[hbm] * 6, out_s...  2.07 us

profile of v6, /device:TPU:1, one launch (start us, length us, event | category | flops | bytes accessed | tf_op | source)
XLA Modules:
  0.0 38.9 jit_solution(3685467053669682792)
XLA Ops:
  0.6 36.2 %shard_map.154 = (f32[512,128]{1,0:T(8,128)}, bf16[512,128]{1,0:T(8,128)(2,1)}, f32[512,128]{1,0:T(8,128)}, f32[128,256]{1,0:T(8,128)}, f32[256,256]{1,0:T(8,128)}, /*index=5*/f32[256,128]{1,0:T(8,128)}) custom-call(f32[512,128]{1,0:T(8,128)} %bitcast.15, f32[512,128]{1,0:T(8,128)} %bitcast.16, f32[128,128]{1,0:T(8,128)} %bitcast.18, f32[128,128]{1,0:T(8,128)} %bitcast.19, ...), custom_call_target="tpu_custom_call" | custom-call | tf_op jit(solution)/shard_map/pallas_call | solution.py:555
  36.8 2.1 %shard_map.155 = (f32[512,128]{1,0:T(8,128)}, bf16[512,128]{1,0:T(8,128)(2,1)}, f32[512,128]{1,0:T(8,128)}, f32[128,256]{1,0:T(8,128)}, f32[256,256]{1,0:T(8,128)}, /*index=5*/f32[256,128]{1,0:T(8,128)}) custom-call(f32[512,128]{1,0:T(8,128)} %get-tuple-element.18.refs_0_, bf16[512,128]{1,0:T(8,128)(2,1)} %get-tuple-element.19.refs_1_, ...), custom_call_target="tpu_custom_call" | custom-call | tf_op jit(solution)/shard_map/pallas_call | solution.py:588
